TPU v7x, 32 devices: a whole 2x2x4 slice. The times are simulated.
32 devices in a mesh: batch: 8 (over y, x, core), field: 4 (over z).
Axes of the slice: x: 2, y: 2, z: 4, core: 2. Of those that a mesh axis runs over, the one named last changes fastest.
Arguments:
- inputs: bfloat16 [65536, 512], P('batch', 'field'), may hold values from -6 to 6
- labels: int32 [65536, 2], P(('batch', 'field')), may hold values 0 or 1
- user_ids: int32 [65536], P(('batch', 'field')), may hold values from 0 to 16383
- first_weight: float32 [512, 2048], P('field'), may hold values from -0.25 to 0.25
- first_mean: float32 [512, 2048], P('field'), may hold values from -28 to 28
- first_square: float32 [512, 2048], P('field'), may hold values from 1.048576 to 17.03936
- gate_weight: float32 [512, 16], P('field'), may hold values from -0.125 to 0.125
- gate_mean: float32 [512, 16], P('field'), may hold values from -224 to 224
- gate_square: float32 [512, 16], P('field'), may hold values from 72.0896 to 1179.648
- second_weight: float32 [2048, 128], replicated, may hold values from -0.375 to 0.375
- second_mean: float32 [2048, 128], replicated, may hold values from -40 to 40
- second_square: float32 [2048, 128], replicated, may hold values from 1.96608 to 32.768
- tower_weight: float32 [128, 128], replicated, may hold values from -0.5 to 0.5
- tower_mean: float32 [128, 128], replicated, may hold values from -320 to 320
- tower_square: float32 [128, 128], replicated, may hold values from 131.072 to 2097.152
- head_weight: float32 [128], replicated, may hold values from -0.75 to 0.75
- head_mean: float32 [128], replicated, may hold values from -7168 to 7168
- head_square: float32 [128], replicated, may hold values from 65536 to 1048576
- biases: float32 [3202], replicated, may hold values from -0.625 to 0.625
- bias_mean: float32 [3202], replicated, may hold values from -768 to 768
- bias_square: float32 [3202], replicated, may hold values from 0.65536 to 1048576
- second_average: float32 [2048, 128], replicated, may hold values from -0.375 to 0.375
- tower_average: float32 [128, 128], replicated, may hold values from -0.5 to 0.5
- head_average: float32 [128], replicated, may hold values from -0.75 to 0.75
Outputs:
- predicted: float32 [65536, 2], P(('batch', 'field'))
- input_grad: float32 [65536, 512], P('batch', 'field')
- updated_first: float32 [512, 2048], P('field')
- moment_first: float32 [512, 2048], P('field')
- square_first: float32 [512, 2048], P('field')
- updated_gate: float32 [512, 16], P('field')
- moment_gate: float32 [512, 16], P('field')
- square_gate: float32 [512, 16], P('field')
- updated_second: float32 [2048, 128], replicated
- moment_second: float32 [2048, 128], replicated
- square_second: float32 [2048, 128], replicated
- updated_tower: float32 [128, 128], replicated
- moment_tower: float32 [128, 128], replicated
- square_tower: float32 [128, 128], replicated
- updated_head: float32 [128], replicated
- moment_head: float32 [128], replicated
- square_head: float32 [128], replicated
- updated_bias: float32 [3202], replicated
- moment_bias: float32 [3202], replicated
- square_bias: float32 [3202], replicated
- average_second: float32 [2048, 128], replicated
- average_tower: float32 [128, 128], replicated
- average_head: float32 [128], replicated
Inputs may be any that keep to these rules, and one draw needn't show every extreme that they name: `user_ids`: each impression's user.
All inputs are finite; a program needn't handle non-finite values. No bound on the sum of `labels` on one device may be relied on, other than what follows from the above.
Results may differ from a plain program's by a relative error of at most 0.012.
The roundings to bfloat16 on the way count: a program that leaves them out, or rounds other values in their place, can miss the bound.
Values may be sent and summed in bfloat16 or wider, within the bound.
No kernel may reach another device: no remote copies, remote signals or barrier semaphores. Data moves between devices by JAX's collectives and lax.ppermute only.
A program may use at most 192 MiB of HBM per device.

v0:
```python
import jax
import jax.numpy as jnp
from jax import lax
from jax.sharding import PartitionSpec as P

EXPERTS = 8
EXP_H1 = 256
EXP_H2 = 128
TASKS = 2
TOWER = 64
BLOCK_ROWS = 4096
USER_ROWS = 4
STEP = 10
H1 = 2048
H2 = 1024


beta_one = 0.9
beta_two = 0.999
learn_rate = 0.1
decay_rate = 0.01
adam_eps = 1e-08
average_rate = 0.8
loss_scale = 512.0


def silu_slope(values):
    logistic = jax.nn.sigmoid(values)
    return logistic * (1.0 + values * (1.0 - logistic))


def adamw(weight, moment, square, gradient):
    new_moment = beta_one * moment + (1.0 - beta_one) * gradient
    new_square = beta_two * square + (1.0 - beta_two) * gradient * gradient
    moment_hat = new_moment / (1.0 - beta_one**STEP)
    square_hat = new_square / (1.0 - beta_two**STEP)
    new_weight = weight - learn_rate * (
        moment_hat / (jnp.sqrt(square_hat) + adam_eps) + decay_rate * weight
    )
    return (new_weight, new_moment, new_square)


def blend(average, weight):
    return average_rate * average + (1.0 - average_rate) * weight


def on_device(
    inputs,
    labels,
    user_ids,
    first_weight,
    first_mean,
    first_square,
    gate_weight,
    gate_mean,
    gate_square,
    second_weight,
    second_mean,
    second_square,
    tower_weight,
    tower_mean,
    tower_square,
    head_weight,
    head_mean,
    head_square,
    biases,
    bias_mean,
    bias_square,
    second_average,
    tower_average,
    head_average,
):
    nfield = lax.axis_size("field")
    rows_dev, columns = inputs.shape
    nblocks = rows_dev // BLOCK_ROWS
    part_rows = BLOCK_ROWS // nfield
    users_total = rows_dev * lax.axis_size("batch") // USER_ROWS
    local_counts = jax.ops.segment_sum(
        jnp.ones(user_ids.shape, jnp.float32), user_ids, num_segments=users_total
    )
    counts = lax.psum(local_counts, ("batch", "field"))
    present = jnp.sum(jnp.where(counts > 0.0, 1.0, 0.0).astype(jnp.float32))
    row_weight = loss_scale * users_total / (present * counts[user_ids])
    first_low = first_weight.astype(jnp.bfloat16)
    gate_low = gate_weight.astype(jnp.bfloat16)
    second_low = second_weight.astype(jnp.bfloat16).reshape(EXPERTS, EXP_H1, EXP_H2)
    tower_low = tower_weight.astype(jnp.bfloat16).reshape(EXP_H2, TASKS, TOWER)
    head_rows = head_weight.reshape(TASKS, TOWER)
    bias_first = biases[:H1]
    bias_second = biases[H1 : H1 + H2].reshape(EXPERTS, EXP_H2)
    bias_tower = biases[H1 + H2 : H1 + H2 + TASKS * TOWER].reshape(TASKS, TOWER)
    bias_head = biases[H1 + H2 + TASKS * TOWER :]
    blocks_in = inputs.reshape(nfield, nblocks, part_rows, columns)
    targets = labels.astype(jnp.float32).reshape(nblocks, part_rows, TASKS)
    weights_rows = row_weight.reshape(nblocks, part_rows)

    def upper_pass(pre_one, logits, target_rows, weight_rows):
        hidden_one = jax.nn.silu(pre_one).astype(jnp.bfloat16).reshape(part_rows, EXPERTS, EXP_H1)
        pre_two = (
            jnp.einsum("rei,eio->reo", hidden_one, second_low, preferred_element_type=jnp.float32)
            + bias_second
        )
        hidden_two = jax.nn.silu(pre_two)
        gate_values = jax.nn.softmax(logits.reshape(part_rows, TASKS, EXPERTS), axis=-1)
        mixed_rows = jnp.sum(gate_values[:, :, :, None] * hidden_two[:, None], axis=2).astype(
            jnp.bfloat16
        )
        pre_tower = (
            jnp.einsum("rko,okj->rkj", mixed_rows, tower_low, preferred_element_type=jnp.float32)
            + bias_tower
        )
        upper_act = jax.nn.silu(pre_tower)
        logit_rows = jnp.sum(upper_act * head_rows, axis=-1) + bias_head
        prob_rows = jax.nn.sigmoid(logit_rows)
        d_logit = weight_rows[:, None] * (prob_rows - target_rows)
        g_head = jnp.sum(d_logit[:, :, None] * upper_act, axis=0)
        g_bhead = jnp.sum(d_logit, axis=0)
        d_tower = (d_logit[:, :, None] * head_rows * silu_slope(pre_tower)).astype(jnp.bfloat16)
        g_btower = jnp.sum(d_tower.astype(jnp.float32), axis=0)
        g_tower = jnp.einsum(
            "rko,rkj->okj", mixed_rows, d_tower, preferred_element_type=jnp.float32
        )
        d_mixed = jnp.einsum("rkj,okj->rko", d_tower, tower_low, preferred_element_type=jnp.float32)
        d_gates = jnp.sum(d_mixed[:, :, None, :] * hidden_two[:, None], axis=-1)
        centered = d_gates - jnp.sum(gate_values * d_gates, axis=-1, keepdims=True)
        d_logits = (gate_values * centered).astype(jnp.bfloat16).reshape(part_rows, TASKS * EXPERTS)
        d_hidden_two = jnp.sum(gate_values[:, :, :, None] * d_mixed[:, :, None, :], axis=1)
        d_two = (d_hidden_two * silu_slope(pre_two)).astype(jnp.bfloat16)
        g_bsecond = jnp.sum(d_two.astype(jnp.float32), axis=0).reshape(H2)
        g_second = jnp.einsum("rei,reo->eio", hidden_one, d_two, preferred_element_type=jnp.float32)
        d_hidden_one = jnp.einsum(
            "reo,eio->rei", d_two, second_low, preferred_element_type=jnp.float32
        ).reshape(part_rows, H1)
        d_one = (d_hidden_one * silu_slope(pre_one)).astype(jnp.bfloat16)
        g_bfirst = jnp.sum(d_one.astype(jnp.float32), axis=0)
        g_bias = jnp.concatenate([g_bfirst, g_bsecond, g_btower.reshape(TASKS * TOWER), g_bhead])
        dense_grads = (
            g_second.reshape(H1, EXP_H2),
            g_tower.reshape(EXP_H2, TASKS * TOWER),
            g_head.reshape(TASKS * TOWER),
            g_bias,
        )
        return (prob_rows, d_one, d_logits, dense_grads)

    def block_step(totals, block_index):
        block_in = lax.dynamic_index_in_dim(blocks_in, block_index, 1, keepdims=False).reshape(
            BLOCK_ROWS, columns
        )
        target_rows = lax.dynamic_index_in_dim(targets, block_index, 0, keepdims=False)
        weight_rows = lax.dynamic_index_in_dim(weights_rows, block_index, 0, keepdims=False)
        pre_part = jnp.dot(block_in, first_low, preferred_element_type=jnp.float32)
        gate_part = jnp.dot(block_in, gate_low, preferred_element_type=jnp.float32)
        pre_one, logits = (
            lax.psum_scatter(pre_part, "field", scatter_dimension=0, tiled=True),
            lax.psum_scatter(gate_part, "field", scatter_dimension=0, tiled=True),
        )
        pre_one = pre_one + bias_first
        prob_rows, d_one, d_logits, dense_grads = upper_pass(
            pre_one, logits, target_rows, weight_rows
        )
        d_all, d_gate_all = (
            lax.all_gather(d_one, "field", axis=0, tiled=True),
            lax.all_gather(d_logits, "field", axis=0, tiled=True),
        )
        block_grads = jnp.dot(d_all, first_low.T, preferred_element_type=jnp.float32) + jnp.dot(
            d_gate_all, gate_low.T, preferred_element_type=jnp.float32
        )
        g_first = jnp.dot(block_in.T, d_all, preferred_element_type=jnp.float32)
        g_gate = jnp.dot(block_in.T, d_gate_all, preferred_element_type=jnp.float32)
        totals = jax.tree.map(jnp.add, totals, (g_first, g_gate) + dense_grads)
        return (totals, (prob_rows, block_grads))

    zeros = (
        jnp.zeros((columns, H1), jnp.float32),
        jnp.zeros((columns, TASKS * EXPERTS), jnp.float32),
        jnp.zeros((H1, EXP_H2), jnp.float32),
        jnp.zeros((EXP_H2, TASKS * TOWER), jnp.float32),
        jnp.zeros((TASKS * TOWER,), jnp.float32),
        jnp.zeros(biases.shape, jnp.float32),
    )
    totals, (probs, grads_out) = lax.scan(block_step, zeros, jnp.arange(nblocks, dtype=jnp.int32))
    predicted = probs.reshape(nblocks * part_rows, TASKS)
    input_grad = (
        grads_out.reshape(nblocks, nfield, part_rows, columns)
        .transpose(1, 0, 2, 3)
        .reshape(rows_dev, columns)
    )
    g_first, g_gate, g_second, g_tower, g_head, g_bias = totals
    g_first, g_gate = lax.psum((g_first, g_gate), "batch")
    g_second, g_tower, g_head, g_bias = lax.psum(
        (g_second, g_tower, g_head, g_bias), ("batch", "field")
    )
    new_first = adamw(first_weight, first_mean, first_square, g_first)
    new_gate = adamw(gate_weight, gate_mean, gate_square, g_gate)
    new_second = adamw(second_weight, second_mean, second_square, g_second)
    new_tower = adamw(tower_weight, tower_mean, tower_square, g_tower)
    avg_second = blend(second_average, new_second[0])
    avg_tower = blend(tower_average, new_tower[0])
    new_head = adamw(head_weight, head_mean, head_square, g_head)
    new_bias = adamw(biases, bias_mean, bias_square, g_bias)
    avg_head = blend(head_average, new_head[0])
    return (
        predicted,
        input_grad,
        new_first[0],
        new_first[1],
        new_first[2],
        new_gate[0],
        new_gate[1],
        new_gate[2],
        new_second[0],
        new_second[1],
        new_second[2],
        new_tower[0],
        new_tower[1],
        new_tower[2],
        new_head[0],
        new_head[1],
        new_head[2],
        new_bias[0],
        new_bias[1],
        new_bias[2],
        avg_second,
        avg_tower,
        avg_head,
    )


def solution(mesh):
    in_specs = (
        P("batch", "field"),
        P(("batch", "field"), None),
        P(("batch", "field")),
        P("field", None),
        P("field", None),
        P("field", None),
        P("field", None),
        P("field", None),
        P("field", None),
        P(),
        P(),
        P(),
        P(),
        P(),
        P(),
        P(),
        P(),
        P(),
        P(),
        P(),
        P(),
        P(),
        P(),
        P(),
    )
    out_specs = (
        P(("batch", "field"), None),
        P("batch", "field"),
        P("field", None),
        P("field", None),
        P("field", None),
        P("field", None),
        P("field", None),
        P("field", None),
        P(),
        P(),
        P(),
        P(),
        P(),
        P(),
        P(),
        P(),
        P(),
        P(),
        P(),
        P(),
        P(),
        P(),
        P(),
    )
    return jax.shard_map(
        on_device, mesh=mesh, in_specs=in_specs, out_specs=out_specs, check_vma=False
    )
```

profile of v0, /device:TPU:0, one launch (start us, length us, event | category | flops | bytes accessed | tf_op | source)
XLA Modules:
  0.0 2252.5 jit_solution(5278714285426310822)
XLA Ops:
  7.2 12.0 scatter_custom_fusion
  22.8 2.1 convert_element_type.44
  24.9 2.1 convert_element_type.45
  28.6 111.0 %all-reduce.6.cloned.1.call-done = f32[16384]{0:T(1024)} async-done(((f32[16384]{0:T(1024)}), f32[16384]{0:T(1024)}) %all-reduce.6.cloned.1.call-update) | async-done | bytes 65552 | tf_op jit(solution)/shard_map/psum | solution.py:81
  139.6 1.5 select_reduce_fusion
  141.2 11.8 gather_fusion
  153.7 1890.8 %while.25 = (s32[]{:T(128)}, f32[128,2048]{1,0:T(8,128)}, f32[128,16]{0,1:T(8,128)}, f32[2048,128]{1,0:T(8,128)}, f32[128,128]{0,1:T(8,128)}, /*index=5*/f32[128...) while((s32[]{:T(128)}, f32[128,2048]{1,0:T(8,128)}, ...), condition=%wide.region_18.19_spmd.clone, body=%wide.region_3.18_spmd.clone.sunk | while | flops 8275638784 | bytes 505296384 | solution.py:181
  158.8 14.2 fusion.126
  173.3 6.1 reduce-scatter.5.cloned.1.call-done
  182.6 14.4 fusion.128
  197.8 5.6 fusion.129
  203.4 528.7 %reduce-scatter.3.cloned.1.call-done = f32[1024,2048]{1,0:T(8,128)} async-done(((f32[4096,2048]{1,0:T(8,128)}), f32[1024,2048]{1,0:T(8,128)}) %reduce-scatter.3.cloned.1.call-update) | async-done | bytes 8388624 | tf_op jit(solution)/shard_map/while/body/eval_jaxpr/reduce_scatter | solution.py:154
  732.1 5.9 multiply_convert_fusion.6
  738.0 6.4 copy.124
  744.4 4.3 bitcast_multiply_fusion.4
  748.7 2.4 copy.125
  751.1 6.4 multiply_reduce_fusion.10
  760.8 6.0 multiply_reduce_fusion.12
  766.8 2.5 convert_reduce_fusion.7
  769.4 4.5 fusion.131
  773.9 9.2 copy.129
  783.1 9.4 convert_reduce_fusion.8
  792.5 1.9 copy.131
  794.4 16.6 multiply_reduce_fusion.13
  811.0 2.4 broadcast_subtract_fusion.2
  815.9 21.1 all_gather.11
  837.5 1.4 divide_dynamic-update-slice_fusion.2
  843.0 4.1 fusion.133
  847.4 234.9 %all-gather.2.cloned.1.call-done = bf16[4096,2048]{1,0:T(8,128)(2,1)} async-done(((bf16[1024,2048]{1,0:T(8,128)(2,1)}), bf16[4096,2048]{1,0:T(8,128)(2,1)}) %all-gather.2.cloned.1.call-update) | async-done | bytes 16777232 | tf_op jit(solution)/shard_map/while/body/eval_jaxpr/all_gather | solution.py:162
  1082.2 10.2 fusion.136
  1092.5 2.6 fusion.137
  1095.2 2.5 convolution_add_fusion.6
  1103.9 14.2 fusion.126
  1118.3 3.5 reduce-scatter.5.cloned.1.call-done
  1125.0 14.4 fusion.128
  1140.2 5.6 fusion.129
  1145.8 528.6 %reduce-scatter.3.cloned.1.call-done = f32[1024,2048]{1,0:T(8,128)} async-done(((f32[4096,2048]{1,0:T(8,128)}), f32[1024,2048]{1,0:T(8,128)}) %reduce-scatter.3.cloned.1.call-update) | async-done | bytes 8388624 | tf_op jit(solution)/shard_map/while/body/eval_jaxpr/reduce_scatter | solution.py:154
  1674.4 5.9 multiply_convert_fusion.6
  1680.3 6.4 copy.124
  1686.7 4.3 bitcast_multiply_fusion.4
  1691.0 2.4 copy.125
  1693.4 6.4 multiply_reduce_fusion.10
  1703.1 6.0 multiply_reduce_fusion.12
  1709.2 2.5 convert_reduce_fusion.7
  1711.7 4.5 fusion.131
  1716.2 9.2 copy.129
  1725.4 9.4 convert_reduce_fusion.8
  1734.8 1.9 copy.131
  1736.7 16.6 multiply_reduce_fusion.13
  1753.3 2.4 broadcast_subtract_fusion.2
  1758.2 21.0 all_gather.11
  1784.5 1.5 bitcast_add_fusion.6
  1786.0 1.6 convolution_add_fusion.7
  1787.6 4.2 fusion.133
  1792.0 232.5 %all-gather.2.cloned.1.call-done = bf16[4096,2048]{1,0:T(8,128)(2,1)} async-done(((bf16[1024,2048]{1,0:T(8,128)(2,1)}), bf16[4096,2048]{1,0:T(8,128)(2,1)}) %all-gather.2.cloned.1.call-update) | async-done | bytes 16777232 | tf_op jit(solution)/shard_map/while/body/eval_jaxpr/all_gather | solution.py:162
  2024.5 10.2 fusion.136
  2034.7 2.6 fusion.137
  2037.4 2.5 convolution_add_fusion.6
  2045.4 4.7 copy.98
  2050.8 38.6 %all-reduce = (f32[128]{0:T(128)S(1)}, f32[3202]{0:T(1024)S(1)}) all-reduce(f32[128]{0:T(128)S(1)} %copy-done.42, f32[3202]{0:T(1024)S(1)} %copy-done.21), channel_id=1, replica_groups=mesh['batch'=8,'field'=4] {'batch','field'}, use_global_device_ids=true, to_apply=%region_23.24 | all-reduce | flops 3330 | bytes 26640 | tf_op jit(solution)/shard_map/psum | solution.py:190
  2089.5 13.2 psum.51
  2104.6 3.8 multiply_subtract_fusion.1
  2108.4 131.6 %all-reduce.10.cloned.1.call-done = (f32[2048,128]{1,0:T(8,128)}, f32[128,128]{1,0:T(8,128)}) async-done(((f32[2048,128]{1,0:T(8,128)}, f32[128,128]{1,0:T(8,128)}), (f32[2048,128]{1,0:T(8,128)}, f32[128,128]{1,0:T(8,128)})) %all-reduce.10.cloned.1.call-update) | async-done | bytes 1114128 | tf_op jit(solution)/shard_map/psum | solution.py:190
  2240.0 4.8 multiply_add_fusion
  (265 shorter events, 48.6 us)
Async XLA Ops:
  7.2 132.5 %all-reduce.6.cloned.1.call-start = ((), (), s32[]{:S(2)}) async-start(), calls=%async_computation.2 | async-start | bytes 131072 | tf_op jit(solution)/shard_map/psum | solution.py:81
  141.2 12.5 slice-start
  141.2 12.5 copy-start.47
  153.7 19.4 copy-start.22
  153.7 19.4 copy-start.53
  153.7 19.5 copy-start.39
  153.7 19.6 copy-start.30
  153.7 604.2 %copy-start.26 = (f32[2,1024,2]{1,2,0:T(2,128)}, f32[2,1024,2]{1,2,0:T(2,128)S(1)}, u32[]{:S(2)}) copy-start(f32[2,1024,2]{1,2,0:T(2,128)S(1)} %get-tuple-element.537) | copy-start | bytes 49156 | tf_op jit(solution)/shard_map/while
  153.7 604.2 %copy-start.36 = (f32[2]{0:T(128)}, f32[2]{0:T(128)S(1)}, u32[]{:S(2)}) copy-start(f32[2]{0:T(128)S(1)} %get-tuple-element.536) | copy-start | bytes 28 | tf_op jit(solution)/shard_map/while
  153.8 605.9 %copy-start.17 = (bf16[128,2,64]{0,2,1:T(8,128)(2,1)}, bf16[128,2,64]{0,2,1:T(8,128)(2,1)S(1)}, u32[]{:S(2)}) copy-start(bf16[128,2,64]{0,2,1:T(8,128)(2,1)S(1)} %get-tuple-element.533) | copy-start | bytes 98308 | tf_op jit(solution)/shard_map/while
  153.8 613.1 %copy-start.28 = (f32[1024]{0:T(1024)}, f32[1024]{0:T(1024)S(1)}, u32[]{:S(2)}) copy-start(f32[1024]{0:T(1024)S(1)} %get-tuple-element.532) | copy-start | bytes 12292 | tf_op jit(solution)/shard_map/while
  153.8 25.6 %reduce-scatter.5.cloned.1.call-start = ((), (), s32[]{:S(2)}) async-start(), calls=%async_computation.6 | async-start | bytes 327680 | tf_op jit(solution)/shard_map/while/body/eval_jaxpr/reduce_scatter | solution.py:155
  158.8 573.3 %reduce-scatter.3.cloned.1.call-start = ((), (), s32[]{:S(2)}) async-start(), calls=%async_computation.5 | async-start | bytes 41943040 | tf_op jit(solution)/shard_map/while/body/eval_jaxpr/reduce_scatter | solution.py:154
  173.1 909.1 %all-gather.2.cloned.1.call-start = ((), (), s32[]{:S(2)}) async-start(), calls=%async_computation.7 | async-start | bytes 20971520 | tf_op jit(solution)/shard_map/while/body/eval_jaxpr/all_gather | solution.py:162
  203.4 547.7 %copy-start.2 = (f32[1024,2,8]{2,1,0:T(2,128)}, f32[1024,2,8]{2,1,0:T(2,128)S(1)}, u32[]{:S(2)}) copy-start(f32[1024,2,8]{2,1,0:T(2,128)S(1)} %fusion.129) | copy-start | bytes 196612 | tf_op jit(solution)/shard_map/while
  757.9 8.9 copy-start.20
  769.4 4.5 copy-start.6
  792.5 22.7 %copy-start.12 = (f32[1024,16]{0,1:T(8,128)S(1)}, f32[1024,16]{0,1:T(8,128)}, u32[]{:S(2)}) copy-start(f32[1024,16]{0,1:T(8,128)} %reduce-scatter.5.cloned.1.call-done) | copy-start | bytes 196612 | tf_op jit(solution)/shard_map/while
  842.2 5.0 copy-start.9
  847.4 245.1 %copy-start.10 = (f32[2048,128]{1,0:T(8,128)}, f32[2048,128]{1,0:T(8,128)S(1)}, u32[]{:S(2)}) copy-start(f32[2048,128]{1,0:T(8,128)S(1)} %bitcast_add_fusion.5) | copy-start | bytes 3145732 | tf_op jit(solution)/shard_map/while
  1082.2 12.8 copy-start.1
  1095.1 3.6 copy-start.23
  1098.7 19.4 copy-start.22
  1098.7 19.3 copy-start.53
  1098.7 19.5 copy-start.39
  1098.7 19.6 copy-start.30
  1098.8 601.5 %copy-start.26 = (f32[2,1024,2]{1,2,0:T(2,128)}, f32[2,1024,2]{1,2,0:T(2,128)S(1)}, u32[]{:S(2)}) copy-start(f32[2,1024,2]{1,2,0:T(2,128)S(1)} %get-tuple-element.537) | copy-start | bytes 49156 | tf_op jit(solution)/shard_map/while
  1098.8 601.5 %copy-start.36 = (f32[2]{0:T(128)}, f32[2]{0:T(128)S(1)}, u32[]{:S(2)}) copy-start(f32[2]{0:T(128)S(1)} %get-tuple-element.536) | copy-start | bytes 28 | tf_op jit(solution)/shard_map/while
  1098.8 603.1 %copy-start.17 = (bf16[128,2,64]{0,2,1:T(8,128)(2,1)}, bf16[128,2,64]{0,2,1:T(8,128)(2,1)S(1)}, u32[]{:S(2)}) copy-start(bf16[128,2,64]{0,2,1:T(8,128)(2,1)S(1)} %get-tuple-element.533) | copy-start | bytes 98308 | tf_op jit(solution)/shard_map/while
  1098.8 610.3 %copy-start.28 = (f32[1024]{0:T(1024)}, f32[1024]{0:T(1024)S(1)}, u32[]{:S(2)}) copy-start(f32[1024]{0:T(1024)S(1)} %get-tuple-element.532) | copy-start | bytes 12292 | tf_op jit(solution)/shard_map/while
  1098.8 23.0 %reduce-scatter.5.cloned.1.call-start = ((), (), s32[]{:S(2)}) async-start(), calls=%async_computation.6 | async-start | bytes 327680 | tf_op jit(solution)/shard_map/while/body/eval_jaxpr/reduce_scatter | solution.py:155
  1103.8 570.6 %reduce-scatter.3.cloned.1.call-start = ((), (), s32[]{:S(2)}) async-start(), calls=%async_computation.5 | async-start | bytes 41943040 | tf_op jit(solution)/shard_map/while/body/eval_jaxpr/reduce_scatter | solution.py:154
  1118.1 906.4 %all-gather.2.cloned.1.call-start = ((), (), s32[]{:S(2)}) async-start(), calls=%async_computation.7 | async-start | bytes 20971520 | tf_op jit(solution)/shard_map/while/body/eval_jaxpr/all_gather | solution.py:162
  1145.8 547.6 %copy-start.2 = (f32[1024,2,8]{2,1,0:T(2,128)}, f32[1024,2,8]{2,1,0:T(2,128)S(1)}, u32[]{:S(2)}) copy-start(f32[1024,2,8]{2,1,0:T(2,128)S(1)} %fusion.129) | copy-start | bytes 196612 | tf_op jit(solution)/shard_map/while
  1700.2 8.9 copy-start.20
  1711.7 4.5 copy-start.6
  1734.8 22.7 %copy-start.12 = (f32[1024,16]{0,1:T(8,128)S(1)}, f32[1024,16]{0,1:T(8,128)}, u32[]{:S(2)}) copy-start(f32[1024,16]{0,1:T(8,128)} %reduce-scatter.5.cloned.1.call-done) | copy-start | bytes 196612 | tf_op jit(solution)/shard_map/while
  1786.0 5.8 copy-start.9
  1792.0 242.7 %copy-start.10 = (f32[2048,128]{1,0:T(8,128)}, f32[2048,128]{1,0:T(8,128)S(1)}, u32[]{:S(2)}) copy-start(f32[2048,128]{1,0:T(8,128)S(1)} %bitcast_add_fusion.5) | copy-start | bytes 3145732 | tf_op jit(solution)/shard_map/while
  2024.5 12.8 copy-start.1
  2044.4 60.1 %all-reduce.8.cloned.1.call-start = ((), (), s32[]{:S(2)}) async-start(), calls=%async_computation.3 | async-start | bytes 2097152 | tf_op jit(solution)/shard_map/psum | solution.py:189
  2045.2 194.8 %all-reduce.10.cloned.1.call-start = ((), (), s32[]{:S(2)}) async-start(), calls=%async_computation.4 | async-start | bytes 2228224 | tf_op jit(solution)/shard_map/psum | solution.py:190
  2045.2 4.9 copy-start.16
  2045.3 5.6 copy-start.21
  2045.3 5.6 copy-start.42
  2045.3 44.2 %copy-start.24 = (f32[128,16]{0,1:T(8,128)S(1)}, f32[128,16]{0,1:T(8,128)}, u32[]{:S(2)}) copy-start(f32[128,16]{0,1:T(8,128)} %get-tuple-element.573) | copy-start | bytes 24580
  2045.3 57.4 %copy-start.41 = (f32[128,16]{0,1:T(8,128)S(1)}, f32[128,16]{0,1:T(8,128)}, u32[]{:S(2)}) copy-start(f32[128,16]{0,1:T(8,128)} %param.32) | copy-start | bytes 24580
  2045.3 57.4 %copy-start.45 = (f32[128,16]{0,1:T(8,128)S(1)}, f32[128,16]{0,1:T(8,128)}, u32[]{:S(2)}) copy-start(f32[128,16]{0,1:T(8,128)} %param.33) | copy-start | bytes 24580
  2045.3 57.4 %copy-start.46 = (f32[128,16]{0,1:T(8,128)S(1)}, f32[128,16]{0,1:T(8,128)}, u32[]{:S(2)}) copy-start(f32[128,16]{0,1:T(8,128)} %param.34) | copy-start | bytes 24580
  2045.3 58.0 %copy-start.38 = (f32[3202]{0:T(1024)S(1)}, f32[3202]{0:T(1024)}, u32[]{:S(2)}) copy-start(f32[3202]{0:T(1024)} %param.44) | copy-start | bytes 38428
  2045.3 58.0 %copy-start.43 = (f32[3202]{0:T(1024)S(1)}, f32[3202]{0:T(1024)}, u32[]{:S(2)}) copy-start(f32[3202]{0:T(1024)} %param.45) | copy-start | bytes 38428
  2045.4 58.0 %copy-start.44 = (f32[3202]{0:T(1024)S(1)}, f32[3202]{0:T(1024)}, u32[]{:S(2)}) copy-start(f32[3202]{0:T(1024)} %param.46) | copy-start | bytes 38428
  2045.4 58.7 %copy-start.49 = (f32[128]{0:T(128)S(1)}, f32[128]{0:T(128)}, u32[]{:S(2)}) copy-start(f32[128]{0:T(128)} %param.41) | copy-start | bytes 1540
  2045.4 58.6 %copy-start.50 = (f32[128]{0:T(128)S(1)}, f32[128]{0:T(128)}, u32[]{:S(2)}) copy-start(f32[128]{0:T(128)} %param.49) | copy-start | bytes 1540
  2045.4 58.6 %copy-start.51 = (f32[128]{0:T(128)S(1)}, f32[128]{0:T(128)}, u32[]{:S(2)}) copy-start(f32[128]{0:T(128)} %param.42) | copy-start | bytes 1540
  2045.4 58.6 %copy-start.52 = (f32[128]{0:T(128)S(1)}, f32[128]{0:T(128)}, u32[]{:S(2)}) copy-start(f32[128]{0:T(128)} %param.43) | copy-start | bytes 1540
  2045.4 59.2 %copy-start.14 = (f32[128,2048]{1,0:T(8,128)S(1)}, f32[128,2048]{1,0:T(8,128)}, u32[]{:S(2)}) copy-start(f32[128,2048]{1,0:T(8,128)} %param.29) | copy-start | bytes 3145732
  2045.4 59.2 %copy-start.19 = (f32[128,2048]{1,0:T(8,128)S(1)}, f32[128,2048]{1,0:T(8,128)}, u32[]{:S(2)}) copy-start(f32[128,2048]{1,0:T(8,128)} %param.30) | copy-start | bytes 3145732
  2103.3 136.6 %copy-start.15 = (f32[2048,128]{1,0:T(8,128)S(1)}, f32[2048,128]{1,0:T(8,128)}, u32[]{:S(2)}) copy-start(f32[2048,128]{1,0:T(8,128)} %param.35) | copy-start | bytes 3145732
  2240.0 4.9 copy-start.25
  2240.0 4.9 copy-start.32
  2240.0 4.9 copy-start.33
  2240.0 4.9 copy-start.34
  2240.0 4.9 copy-start.35
  (32 other events, 88.7 us)
Sparse Core Ops, SparseCore 0:
  19.4 120.2 all-reduce.5
  158.9 20.4 reduce-scatter.4
  181.8 550.2 reduce-scatter.2
  792.6 289.5 all-gather.1
  1103.9 17.8 reduce-scatter.4
  1124.1 550.3 reduce-scatter.2
  1734.9 289.5 all-gather.1
  2049.0 55.2 all-reduce.7
  2110.4 129.5 all-reduce.9
where the time goes:
time: 2280 us; the launch traced here: 2250 us
  waiting for transfers between devices  1780 us (78%)
  other arithmetic  187 us (8%)
  blocking collectives  93.9 us (4%)
  matrix products  93.4 us (4%)
  local copies, waits for them, and re-layouts  77 us (3%)
    reduce_scatter x2, waiting for transfers between devices, block_step(): lax.psum_scatter(pre_part, 'field', scatter_dimension=0, tiled=True)  1060 us
    all_gather x2, waiting for transfers between devices, block_step(): lax.all_gather(d_one, 'field', axis=0, tiled=True)  467 us
    psum x1, waiting for transfers between devices, on_device(): lax.psum((g_second, g_tower, g_head, g_bias), ('batch', 'field'))  132 us
    psum x1, waiting for transfers between devices, on_device(): counts = lax.psum(local_counts, ('batch', 'field'))  111 us
  transfers between devices with their start and end apart: 9, of which 8 were waited for; matrix products, arithmetic and copies ran while one was open for 7% of the time, Pallas kernels for 0%

commit v1 on v0

v1 whole, which is shorter than its diff:
```python
import functools

import jax
import jax.numpy as jnp
from jax import lax
from jax.experimental import pallas as pl
from jax.experimental.pallas import tpu as pltpu
from jax.sharding import PartitionSpec as P

EXPERTS = 8
EXP_H1 = 256
EXP_H2 = 128
TASKS = 2
TOWER = 64
USER_ROWS = 4
STEP = 10
H1 = 2048
H2 = 1024
GATES = TASKS * EXPERTS
LANES = 128
GROUP = 8
CHUNKS = 2
SUB_ROWS = 256
VMEM_BYTES = 56 * 1024 * 1024

beta_one = 0.9
beta_two = 0.999
learn_rate = 0.1
decay_rate = 0.01
adam_eps = 1e-08
average_rate = 0.8
loss_scale = 512.0

f32 = jnp.float32
bf16 = jnp.bfloat16


def sigmoid(values):
    return 0.5 * jnp.tanh(0.5 * values) + 0.5


def dot(left, right):
    return jnp.dot(left, right, preferred_element_type=f32)


def dot_nt(left, right, precision=None):
    return lax.dot_general(
        left, right, (((1,), (1,)), ((), ())), precision=precision, preferred_element_type=f32
    )


def adamw(weight, moment, square, gradient):
    new_moment = beta_one * moment + (1.0 - beta_one) * gradient
    new_square = beta_two * square + (1.0 - beta_two) * gradient * gradient
    moment_hat = new_moment / (1.0 - beta_one**STEP)
    square_hat = new_square / (1.0 - beta_two**STEP)
    new_weight = weight - learn_rate * (
        moment_hat / (jnp.sqrt(square_hat) + adam_eps) + decay_rate * weight
    )
    return (new_weight, new_moment, new_square)


def blend(average, weight):
    return average_rate * average + (1.0 - average_rate) * weight


def params(**kwargs):
    return pltpu.CompilerParams(vmem_limit_bytes=VMEM_BYTES, **kwargs)


def cost(flops, nbytes):
    return pl.CostEstimate(flops=int(flops), bytes_accessed=int(nbytes), transcendentals=0)


def count_kernel(ids_ref, out_ref):
    ids = ids_ref[...]
    width = ids.shape[1]
    high = lax.broadcasted_iota(jnp.int32, (out_ref.shape[0], width), 0)
    low = lax.broadcasted_iota(jnp.int32, (LANES, width), 0)
    one_high = jnp.where(high == ids // LANES, 1.0, 0.0).astype(bf16)
    one_low = jnp.where(low == ids % LANES, 1.0, 0.0).astype(bf16)
    out_ref[...] = dot_nt(one_high, one_low)


def weight_kernel(scale, ids_ref, counts_ref, out_ref):
    ids = ids_ref[...]
    counts = counts_ref[...]
    width = ids.shape[1]
    present = jnp.sum(jnp.where(counts > 0.0, 1.0, 0.0), keepdims=True)
    high = lax.broadcasted_iota(jnp.int32, (counts.shape[0], width), 0)
    low = lax.broadcasted_iota(jnp.int32, (LANES, width), 0)
    one_high = jnp.where(high == ids // LANES, 1.0, 0.0)
    columns = lax.dot_general(
        counts,
        one_high,
        (((0,), (0,)), ((), ())),
        precision=lax.Precision.HIGHEST,
        preferred_element_type=f32,
    )
    mine = jnp.sum(jnp.where(low == ids % LANES, columns, 0.0), axis=0, keepdims=True)
    out_ref[...] = scale / (present * mine)


def prepare_kernel(place_ref, *refs):
    pieces, (first_ref, turned_ref) = refs[:GROUP], refs[GROUP:]
    for slot, piece_ref in enumerate(pieces):
        expert = place_ref[0] ^ slot
        start = pl.multiple_of(expert * EXP_H1, EXP_H1)
        piece = piece_ref[...]
        first_ref[:, pl.ds(start, EXP_H1)] = piece
        turned_ref[pl.ds(start, EXP_H1), :] = piece.T


def layers_kernel(
    last,
    with_sums,
    place_ref,
    x0,
    x1,
    x2,
    x3,
    labels_ref,
    weights_ref,
    turned_ref,
    gate_ref,
    second_ref,
    second_t_ref,
    tower_fwd_ref,
    tower_bwd_ref,
    bias_one_ref,
    bias_two_ref,
    bias_top_ref,
    *rest,
):
    nsum = 5
    sums_in, rest = (rest[:nsum], rest[nsum:]) if with_sums else (None, rest)
    d_ref, prob_ref, rest = rest[0], rest[1], rest[2:]
    if last:
        packed_ref, gate_out_ref, small_ref = rest[:3]
        rest = rest[3:]
        sums, rest = rest[:nsum], rest[nsum:]
    else:
        sums, rest = rest[:nsum], rest[nsum:]
    sum_first, sum_second, sum_tower, sum_bias, sum_top = sums
    hidden_ref, slope_ref, two_ref, slope_two_ref = rest
    rows = SUB_ROWS
    step = pl.program_id(0)

    @pl.when(step == 0)
    def _():
        if with_sums:
            for total, given in zip(sums, sums_in):
                total[...] = given[...]
        else:
            for total in sums:
                total[...] = jnp.zeros_like(total)

    def fold(values):
        out = values[:, :LANES]
        for at in range(LANES, values.shape[1], LANES):
            out = out + values[:, at : at + LANES]
        return out

    def wide(values):
        return jnp.concatenate([values] * (rows // LANES), axis=1)

    inputs = jnp.concatenate([x0[...], x1[...], x2[...], x3[...]], axis=1)
    turned_in = inputs.T
    logits = dot(gate_ref[...], turned_in).reshape(TASKS, EXPERTS, rows)
    shifted = jnp.exp(logits - jnp.max(logits, axis=1, keepdims=True))
    gates = shifted / jnp.sum(shifted, axis=1, keepdims=True)
    mixed = [jnp.zeros((EXP_H2, rows), f32) for _ in range(TASKS)]
    for e in range(EXPERTS):
        one, two = pl.ds(e * EXP_H1, EXP_H1), pl.ds(e * EXP_H2, EXP_H2)
        pre_one = dot(turned_ref[one, :], turned_in) + wide(bias_one_ref[one, :])
        logistic = sigmoid(pre_one)
        hidden = pre_one * logistic
        slope_ref[one, :] = logistic + hidden * (1.0 - logistic)
        hidden_low = hidden.astype(bf16)
        hidden_ref[one, :] = hidden_low
        pre_two = dot(second_t_ref[two, :], hidden_low) + wide(bias_two_ref[two, :])
        logistic = sigmoid(pre_two)
        hidden = pre_two * logistic
        slope_two_ref[two, :] = logistic + hidden * (1.0 - logistic)
        two_ref[two, :] = hidden
        for k in range(TASKS):
            mixed[k] = mixed[k] + gates[k, e : e + 1, :] * hidden
    mixed_low = jnp.concatenate(mixed, axis=0).astype(bf16)
    pre_tower = dot(tower_fwd_ref[...], mixed_low) + wide(bias_top_ref[0])
    logistic = sigmoid(pre_tower)
    upper = pre_tower * logistic
    slope_tower = logistic + upper * (1.0 - logistic)
    head = wide(bias_top_ref[1])
    logit = jnp.sum((upper * head).reshape(TASKS, TOWER, rows), axis=1)
    logit = logit + wide(bias_top_ref[2])[:TASKS, :]
    prob = 1.0 / (1.0 + jnp.exp(-logit))
    prob_ref[...] = prob
    d_logit = weights_ref[...] * (prob - labels_ref[...].astype(f32))
    d_wide = jnp.broadcast_to(d_logit[:, None, :], (TASKS, TOWER, rows)).reshape(LANES, rows)
    d_tower = (d_wide * head * slope_tower).astype(bf16)
    sum_top[0] += fold(d_tower.astype(f32))
    sum_top[1] += fold(d_wide * upper)
    sum_top[2, :TASKS, :] += fold(d_logit)
    sum_tower[...] += dot_nt(mixed_low, d_tower)
    d_mixed = dot(tower_bwd_ref[...], d_tower)
    parts = [d_mixed[k * EXP_H2 : (k + 1) * EXP_H2, :] for k in range(TASKS)]
    d_gates = [[], []]
    for e in range(EXPERTS):
        one, two = pl.ds(e * EXP_H1, EXP_H1), pl.ds(e * EXP_H2, EXP_H2)
        hidden = two_ref[two, :]
        for k in range(TASKS):
            d_gates[k].append(jnp.sum(parts[k] * hidden, axis=0, keepdims=True))
        d_hidden = gates[0, e : e + 1, :] * parts[0] + gates[1, e : e + 1, :] * parts[1]
        d_two = d_hidden * slope_two_ref[two, :]
        sum_bias[pl.ds(H1 + e * EXP_H2, EXP_H2), :] += fold(d_two)
        d_two = d_two.astype(bf16)
        sum_second[one, :] += dot_nt(hidden_ref[one, :], d_two)
        d_one = dot(second_ref[one, :], d_two) * slope_ref[one, :]
        sum_bias[one, :] += fold(d_one)
        d_ref[one, :] = d_one.astype(bf16)
    d_gates = jnp.stack([jnp.concatenate(rows_of, axis=0) for rows_of in d_gates])
    centered = d_gates - jnp.sum(gates * d_gates, axis=1, keepdims=True)
    d_ref[pl.ds(H1, GATES), :] = (gates * centered).reshape(GATES, rows).astype(bf16)
    sum_first[...] += dot(d_ref[...], inputs)

    if last:

        @pl.when(step == pl.num_programs(0) - 1)
        def _():
            place = place_ref[0]
            width = sum_first.shape[1]
            for e in range(EXPERTS):
                one = pl.ds(e * EXP_H1, EXP_H1)
                slot = e ^ place
                packed_ref[slot & 1, slot >> 1, :, :width] = sum_first[one, :].astype(bf16)
                packed_ref[slot & 1, slot >> 1, :, width:] = sum_second[one, :].astype(bf16)
            gate_out_ref[...] = sum_first[pl.ds(H1, GATES), :]
            small_ref[:TOWER * TASKS, :TOWER] = sum_tower[:EXP_H2, :TOWER]
            small_ref[:TOWER * TASKS, TOWER:] = sum_tower[EXP_H2:, TOWER:]
            ones = jnp.ones((8, LANES), f32)
            lines = dot_nt(ones, sum_bias[...], lax.Precision.HIGHEST)
            for row in range((H1 + H2) // LANES):
                small_ref[pl.ds(LANES + row, 1), :] = lines[:1, row * LANES : (row + 1) * LANES]
            at = LANES + (H1 + H2) // LANES
            for k in range(3):
                line = dot_nt(ones, sum_top[k], lax.Precision.HIGHEST)
                small_ref[pl.ds(at + k, 1), :] = line[:1, :]
            small_ref[at + 3 :, :] = jnp.zeros((small_ref.shape[0] - at - 3, LANES), f32)


def back_kernel(d_ref, first_ref, gate_ref, own_ref, *others):
    turned = dot(first_ref[...], d_ref[:H1, :]) + dot(gate_ref[...], d_ref[H1:, :])
    grads = turned.T
    width = own_ref.shape[1]
    own_ref[...] = grads[:, :width]
    for s, ref in enumerate(others):
        ref[...] = grads[:, (s + 1) * width : (s + 2) * width].astype(bf16)


def update_kernel(
    place_ref,
    grads_ref,
    first_w,
    first_m,
    first_v,
    second_w,
    second_m,
    second_v,
    second_a,
    first_w_out,
    first_m_out,
    first_v_out,
    second_w_out,
    second_m_out,
    second_v_out,
    second_a_out,
):
    grads = grads_ref[0].astype(f32)
    width = first_w.shape[0]
    new = adamw(first_w[...], first_m[...], first_v[...], grads[:, :width].T)
    first_w_out[...], first_m_out[...], first_v_out[...] = new
    new = adamw(second_w[...], second_m[...], second_v[...], grads[:, width:])
    second_w_out[...], second_m_out[...], second_v_out[...] = new
    second_a_out[...] = blend(second_a[...], new[0])


def on_device(
    inputs,
    labels,
    user_ids,
    first_weight,
    first_mean,
    first_square,
    gate_weight,
    gate_mean,
    gate_square,
    second_weight,
    second_mean,
    second_square,
    tower_weight,
    tower_mean,
    tower_square,
    head_weight,
    head_mean,
    head_square,
    biases,
    bias_mean,
    bias_square,
    second_average,
    tower_average,
    head_average,
):
    nfield, nbatch = lax.axis_size("field"), lax.axis_size("batch")
    field, batch = lax.axis_index("field"), lax.axis_index("batch")
    rows_dev, columns = inputs.shape
    rows = rows_dev // nfield
    chunk = rows // CHUNKS
    users_total = rows_dev * nbatch // USER_ROWS
    place = (batch % GROUP).astype(jnp.int32)
    place_arg = place.reshape(1)

    def shift(value, by):
        return lax.ppermute(value, "field", [(i, (i + by) % nfield) for i in range(nfield)])

    def cross(value, mask):
        return lax.ppermute(value, "batch", [(i, i ^ mask) for i in range(nbatch)])

    def sum_field(value):
        hop = 1
        while hop < nfield:
            value = value + lax.ppermute(value, "field", [(i, i ^ hop) for i in range(nfield)])
            hop *= 2
        return value

    def sum_batch(value):
        hop = 1
        while hop < nbatch:
            value = value + cross(value, hop)
            hop *= 2
        return value

    smem = pl.BlockSpec(memory_space=pltpu.SMEM)
    whole = pl.BlockSpec(memory_space=pltpu.VMEM)

    first_low = first_weight.astype(bf16)
    gate_low = gate_weight.astype(bf16)
    piece = lax.dynamic_slice_in_dim(first_low, place * EXP_H1, EXP_H1, 1)
    bundle = jnp.concatenate([piece] + [shift(piece, s) for s in range(1, nfield)], axis=0)
    gate_t = gate_low.T
    gate_t = jnp.concatenate([gate_t] + [shift(gate_t, s) for s in range(1, nfield)], axis=1)
    even = [bundle] + [cross(bundle, 2 * j) for j in range(1, GROUP // 2)]
    odd = [cross(part, 1) for part in even]
    slots = [part for pair in zip(even, odd) for part in pair]

    ids = user_ids.reshape(1, rows)
    counts = pl.pallas_call(
        count_kernel,
        out_shape=jax.ShapeDtypeStruct((users_total // LANES, LANES), f32),
        in_specs=[whole],
        out_specs=whole,
        compiler_params=params(),
        name="user_counts",
    )(ids)
    counts = sum_field(sum_batch(counts))
    row_weight = pl.pallas_call(
        functools.partial(weight_kernel, loss_scale * users_total),
        out_shape=jax.ShapeDtypeStruct((1, rows), f32),
        in_specs=[whole] * 2,
        out_specs=whole,
        compiler_params=params(),
        name="row_weights",
    )(ids, counts)

    first_all, turned_all = pl.pallas_call(
        prepare_kernel,
        out_shape=(
            jax.ShapeDtypeStruct((nfield * columns, H1), bf16),
            jax.ShapeDtypeStruct((H1, nfield * columns), bf16),
        ),
        in_specs=[smem] + [whole] * GROUP,
        out_specs=(whole, whole),
        compiler_params=params(),
        name="prepare_first",
    )(place_arg, *slots)

    second_low = second_weight.astype(bf16)
    second_t = second_low.reshape(EXPERTS, EXP_H1, EXP_H2).transpose(0, 2, 1).reshape(H2, EXP_H1)
    tower_low = tower_weight.astype(bf16)
    none = jnp.zeros((EXP_H2, TOWER), bf16)
    tower_bwd = jnp.concatenate(
        [
            jnp.concatenate([tower_low[:, :TOWER], none], axis=1),
            jnp.concatenate([none, tower_low[:, TOWER:]], axis=1),
        ],
        axis=0,
    )
    tower_fwd = tower_bwd.T
    bias_one = jnp.broadcast_to(biases[:H1, None], (H1, LANES))
    bias_two = jnp.broadcast_to(biases[H1 : H1 + H2, None], (H2, LANES))
    top = jnp.stack(
        [
            biases[H1 + H2 : H1 + H2 + LANES],
            head_weight,
            jnp.pad(biases[H1 + H2 + LANES :], (0, LANES - TASKS)),
        ]
    )
    bias_top = jnp.broadcast_to(top[:, :, None], (3, LANES, LANES))
    labels_t = labels.T

    def chunk_rows(c, s):
        start = (field + s) % nfield * rows + c * chunk
        return lax.dynamic_slice_in_dim(inputs, start, chunk, 0)

    arrived = []
    for c in range(CHUNKS):
        arrived.append(
            [chunk_rows(c, 0)] + [shift(chunk_rows(c, s), s) for s in range(1, nfield)]
        )

    sum_shapes = [
        jax.ShapeDtypeStruct((H1 + GATES, nfield * columns), f32),
        jax.ShapeDtypeStruct((H1, EXP_H2), f32),
        jax.ShapeDtypeStruct((TASKS * EXP_H2, TASKS * TOWER), f32),
        jax.ShapeDtypeStruct((H1 + H2, LANES), f32),
        jax.ShapeDtypeStruct((3, LANES, LANES), f32),
    ]

    def full(shape):
        return pl.BlockSpec(shape, lambda i: (0,) * len(shape))

    def run_layers(c, sums):
        last = c == CHUNKS - 1
        x_spec = pl.BlockSpec((SUB_ROWS, columns), lambda i: (i, 0))
        at = c * chunk // SUB_ROWS
        operands = [
            turned_all,
            gate_t,
            second_low,
            second_t,
            tower_fwd,
            tower_bwd,
            bias_one,
            bias_two,
            bias_top,
        ] + list(sums or [])
        out_shape = [
            jax.ShapeDtypeStruct((H1 + GATES, chunk), bf16),
            jax.ShapeDtypeStruct((TASKS, chunk), f32),
        ]
        out_specs = [
            pl.BlockSpec((H1 + GATES, SUB_ROWS), lambda i: (0, i)),
            pl.BlockSpec((TASKS, SUB_ROWS), lambda i: (0, i)),
        ]
        scratch = [
            pltpu.VMEM((H1, SUB_ROWS), bf16),
            pltpu.VMEM((H1, SUB_ROWS), f32),
            pltpu.VMEM((H2, SUB_ROWS), f32),
            pltpu.VMEM((H2, SUB_ROWS), f32),
        ]
        if last:
            more = [
                jax.ShapeDtypeStruct((2, GROUP // 2, EXP_H1, nfield * columns + EXP_H2), bf16),
                jax.ShapeDtypeStruct((GATES, nfield * columns), f32),
                jax.ShapeDtypeStruct((LANES + 32, LANES), f32),
            ]
            scratch = [pltpu.VMEM(s.shape, s.dtype) for s in sum_shapes] + scratch
        else:
            more = sum_shapes
        out_shape += more
        out_specs += [full(s.shape) for s in more]
        return pl.pallas_call(
            functools.partial(layers_kernel, last, sums is not None),
            grid=(chunk // SUB_ROWS,),
            out_shape=out_shape,
            in_specs=[smem]
            + [x_spec] * nfield
            + [
                pl.BlockSpec((TASKS, SUB_ROWS), lambda i: (0, i + at)),
                pl.BlockSpec((1, SUB_ROWS), lambda i: (0, i + at)),
            ]
            + [full(o.shape) for o in operands],
            out_specs=out_specs,
            scratch_shapes=scratch,
            compiler_params=params(),
            cost_estimate=cost(2 * chunk * 4e6, 20e6),
            name="layers",
        )(place_arg, *arrived[c], labels_t, row_weight, *operands)

    gate_all = gate_t.T

    def run_back(d_chunk):
        block = pl.BlockSpec((SUB_ROWS, columns), lambda i: (i, 0))
        return pl.pallas_call(
            back_kernel,
            grid=(chunk // SUB_ROWS,),
            out_shape=[jax.ShapeDtypeStruct((chunk, columns), f32)]
            + [jax.ShapeDtypeStruct((chunk, columns), bf16)] * (nfield - 1),
            in_specs=[
                pl.BlockSpec((H1 + GATES, SUB_ROWS), lambda i: (0, i)),
                full(first_all.shape),
                full(gate_all.shape),
            ],
            out_specs=[block] * nfield,
            compiler_params=params(),
            cost_estimate=cost(2 * chunk * 1e6, 8e6),
            name="input_gradients",
        )(d_chunk, first_all, gate_all)

    sums = None
    probs = []
    input_grad = jnp.zeros((rows_dev, columns), f32)
    returned = []
    for c in range(CHUNKS):
        d_chunk, prob, *sums = run_layers(c, sums)
        probs.append(prob)
        own, *others = run_back(d_chunk)
        returned.append([own] + [shift(o, -(s + 1)) for s, o in enumerate(others)])
    packed, gate_grad, small = sums

    kept = packed[0].astype(f32) + cross(packed[1], 1).astype(f32)
    kept_low = kept.astype(bf16)
    total = kept[0]
    for j in range(1, GROUP // 2):
        total = total + cross(kept_low[j], 2 * j).astype(f32)
    hop = GROUP
    while hop < nbatch:
        low = total.astype(bf16)
        total = low.astype(f32) + cross(low, hop).astype(f32)
        hop *= 2
    total = total.astype(bf16)
    width = nfield * columns

    def for_field(s):
        return jnp.concatenate([total[:, s * columns : (s + 1) * columns], total[:, width:]], axis=1)

    terms = [for_field(0)] + [shift(for_field(s), -s) for s in range(1, nfield)]
    terms = [t.astype(f32) for t in terms]
    odd_field = field % 2 == 1
    near = jnp.where(odd_field, terms[3], terms[1])
    far = jnp.where(odd_field, terms[1], terms[3])
    done = ((terms[0] + near) + (terms[2] + far)).astype(bf16)
    even = [done] + [cross(done, 2 * j) for j in range(1, GROUP // 2)]
    odd = [cross(part, 1) for part in even]
    grads = jnp.stack([part for pair in zip(even, odd) for part in pair])

    def row_block(j, place_ref):
        return (place_ref[0] ^ j, 0)

    def column_block(j, place_ref):
        return (0, place_ref[0] ^ j)

    first_spec = pl.BlockSpec((columns, EXP_H1), column_block)
    second_spec = pl.BlockSpec((EXP_H1, EXP_H2), row_block)
    updated = pl.pallas_call(
        update_kernel,
        grid_spec=pltpu.PrefetchScalarGridSpec(
            num_scalar_prefetch=1,
            grid=(EXPERTS,),
            in_specs=[pl.BlockSpec((1, EXP_H1, columns + EXP_H2), lambda j, place_ref: (j, 0, 0))]
            + [first_spec] * 3
            + [second_spec] * 4,
            out_specs=[first_spec] * 3 + [second_spec] * 4,
        ),
        out_shape=[jax.ShapeDtypeStruct((columns, H1), f32)] * 3
        + [jax.ShapeDtypeStruct((H1, EXP_H2), f32)] * 4,
        compiler_params=params(),
        cost_estimate=cost(1e6, 15e6),
        name="update_layers",
    )(
        place_arg,
        grads,
        first_weight,
        first_mean,
        first_square,
        second_weight,
        second_mean,
        second_square,
        second_average,
    )
    new_first, new_second, avg_second = updated[:3], updated[3:6], updated[6]

    gate_grad = jnp.concatenate(
        [gate_grad[:, s * columns : (s + 1) * columns] for s in range(nfield)], axis=0
    )
    both = sum_batch(jnp.concatenate([small, gate_grad], axis=0))
    small = sum_field(both[: small.shape[0]])
    gate_grad = both[small.shape[0] :]
    terms = [gate_grad[s * GATES : (s + 1) * GATES] for s in range(nfield)]
    gate_grad = terms[0]
    for s in range(1, nfield):
        gate_grad = gate_grad + shift(terms[s], -s)
    g_tower = small[:LANES]
    lines = (H1 + H2) // LANES
    g_head = small[LANES + lines + 1]
    g_bias = jnp.concatenate(
        [small[LANES : LANES + lines + 1].reshape(-1), small[LANES + lines + 2, :TASKS]]
    )
    new_gate = adamw(gate_weight, gate_mean, gate_square, gate_grad.T)
    new_tower = adamw(tower_weight, tower_mean, tower_square, g_tower)
    avg_tower = blend(tower_average, new_tower[0])
    new_head = adamw(head_weight, head_mean, head_square, g_head)
    avg_head = blend(head_average, new_head[0])
    new_bias = adamw(biases, bias_mean, bias_square, g_bias)

    for c in range(CHUNKS):
        for s in range(nfield):
            start = (field + s) % nfield * rows + c * chunk
            input_grad = lax.dynamic_update_slice_in_dim(
                input_grad, returned[c][s].astype(f32), start, 0
            )
    predicted = jnp.concatenate(probs, axis=1).T
    return (
        predicted,
        input_grad,
        *new_first,
        *new_gate,
        *new_second,
        *new_tower,
        *new_head,
        *new_bias,
        avg_second,
        avg_tower,
        avg_head,
    )


def solution(mesh):
    fields, copied = P("field", None), P()
    rows = P(("batch", "field"), None)
    in_specs = (
        (P("batch", "field"), rows, P(("batch", "field"))) + (fields,) * 6 + (copied,) * 15
    )
    out_specs = (rows, P("batch", "field")) + (fields,) * 6 + (copied,) * 15
    return jax.shard_map(
        on_device, mesh=mesh, in_specs=in_specs, out_specs=out_specs, check_vma=False
    )
```

time: 2280 us -> 255 us (0.11); the launches traced: 2250 us -> 254 us
  waiting for transfers between devices: 1780 us -> 68.9 us
  other arithmetic: 187 us -> 9.35 us
  blocking collectives: 93.9 us -> 0 us
  matrix products: 93.4 us -> 0 us
  Pallas kernels: 0 us -> 77.6 us
  starting transfers between devices: 0.38 us -> 77.1 us
  local copies, waits for them, and re-layouts: 77 us -> 19.1 us
    reduce_scatter x4 -> x0, waiting for transfers between devices: 1070 us -> none  [the longest x2 1060 us: block_step(): lax.psum_scatter(pre_part, 'field', scatter_dimension=0, tiled=True)]
    all_gather x2 -> x0, waiting for transfers between devices: 467 us -> none  [block_step(): lax.all_gather(d_one, 'field', axis=0, tiled=True)]
    psum x3 -> x0, waiting for transfers between devices: 243 us -> none  [the longest x1 132 us: on_device(): lax.psum((g_second, g_tower, g_head, g_bias), ('batch', 'field'))]
    reduce_sum x17 -> x0, other arithmetic: 116 us -> none  [the longest x2 33.2 us: upper_pass(): centered = d_gates - jnp.sum(gate_values * d_gates, axis=-1, keepdims=True)]
    dot_general x24 -> x0, matrix products: 93.4 us -> none  [the longest x2 28.4 us: block_step(): pre_part = jnp.dot(block_in, first_low, preferred_element_type=jnp.float32)]
    pallas_call x0 -> x8, Pallas kernels: none -> 77.6 us  [the longest x2 47.3 us: run_layers(): pl.pallas_call(functools.partial(layers_kernel, last, sums is not None),...]
    ppermute x0 -> x52, starting transfers between devices: none -> 77.1 us  [the longest x24 53.7 us: shift(): lax.ppermute(value, 'field', [(i, (i + by) % nfield) for i in range(nfiel...]
    ppermute x0 -> x52, waiting for transfers between devices: none -> 68.9 us  [the longest x24 41.7 us: shift(): lax.ppermute(value, 'field', [(i, (i + by) % nfield) for i in range(nfiel...]
  transfers between devices with their start and end apart: 9 -> 52, of which waited for: 8 -> 21; matrix products, arithmetic and copies ran while one was open for 7% -> 8% of each run, Pallas kernels for 0% -> 17%
where the time goes in v1:
time: 255 us; the launch traced here: 254 us
  Pallas kernels  77.6 us (30%)
  starting transfers between devices  77.1 us (30%)
  waiting for transfers between devices  68.9 us (27%)
  local copies, waits for them, and re-layouts  19.1 us (7%)
  other arithmetic  9.35 us (4%)
    ppermute x24, starting transfers between devices, shift(): lax.ppermute(value, 'field', [(i, (i + by) % nfield) for i in range(nfiel...  53.7 us
    pallas_call x2, Pallas kernels, run_layers(): pl.pallas_call(functools.partial(layers_kernel, last, sums is not None),...  47.3 us
    ppermute x24, waiting for transfers between devices, shift(): lax.ppermute(value, 'field', [(i, (i + by) % nfield) for i in range(nfiel...  41.7 us
    ppermute x24, waiting for transfers between devices, cross(): return lax.ppermute(value, 'batch', [(i, i ^ mask) for i in range(nbatch)])  25.6 us
    ppermute x24, starting transfers between devices, cross(): return lax.ppermute(value, 'batch', [(i, i ^ mask) for i in range(nbatch)])  15.7 us
    pallas_call x2, Pallas kernels, run_back(): pl.pallas_call(back_kernel, grid=(chunk // SUB_ROWS,), out_shape=[jax.Sha...  12.9 us
    pallas_call x1, Pallas kernels, on_device(): pl.pallas_call(update_kernel, grid_spec=pltpu.PrefetchScalarGridSpec(num_...  9.05 us
    ppermute x4, starting transfers between devices, sum_field(): lax.ppermute(value, 'field', [(i, i ^ hop) for i in range(nfield)])  7.71 us
  transfers between devices with their start and end apart: 52, of which 21 were waited for; matrix products, arithmetic and copies ran while one was open for 8% of the time, Pallas kernels for 17%

profile of v1, /device:TPU:0, one launch (start us, length us, event | category | flops | bytes accessed | tf_op | source)
XLA Modules:
  0.0 253.6 jit_solution(9577741884795610355)
XLA Ops:
  0.7 1.0 dynamic-slice_convert_fusion
  1.7 5.1 %collective-permute-start.10 = (bf16[128,256]{1,0:T(8,128)(2,1)S(1)}, bf16[128,256]{1,0:T(8,128)(2,1)S(1)}, u32[]{:S(2)}, u32[]{:S(2)}) collective-permute-start(bf16[128,256]{1,0:T(8,128)(2,1)S(1)} %dynamic-slice_convert_fusion), channel_id=1, source_target_pairs={{0,3},{1,0},{2,1},{3,2},{4,7},{5,4},{6,5},{7,6},{8,11},{9,8},{10,9... | collective-permute-start | bytes 196616 | tf_op jit(solution)/shard_map/ppermute | solution.py:323
  6.8 1.0 collective-permute-start.9
  7.8 1.6 user_counts.1
  9.5 3.5 %collective-permute-done.8 = bf16[128,256]{1,0:T(8,128)(2,1)S(1)} collective-permute-done((bf16[128,256]{1,0:T(8,128)(2,1)S(1)}, bf16[128,256]{1,0:T(8,128)(2,1)S(1)}, u32[]{:S(2)}, u32[]{:S(2)}) %collective-permute-start.8) | collective-permute-done | bytes 65568 | tf_op jit(solution)/shard_map/ppermute | solution.py:323
  12.9 1.3 collective-permute-done.9
  14.3 1.6 collective-permute-start.12
  15.8 0.8 add.250
  18.0 2.2 collective-permute-start.19
  20.2 1.2 collective-permute-done.4
  21.4 1.6 collective-permute-start.5
  23.0 0.9 broadcast_select_fusion
  25.1 3.8 %collective-permute-done.5 = f32[128,128]{1,0:T(8,128)S(1)} collective-permute-done((f32[128,128]{1,0:T(8,128)S(1)}, f32[128,128]{1,0:T(8,128)S(1)}, u32[]{:S(2)}, u32[]{:S(2)}) %collective-permute-start.5) | collective-permute-done | bytes 65568 | tf_op jit(solution)/shard_map/ppermute | solution.py:326
  28.9 1.9 collective-permute-start.16
  30.9 2.7 %collective-permute-start.6 = (f32[128,128]{1,0:T(8,128)S(1)}, f32[128,128]{1,0:T(8,128)S(1)}, u32[]{:S(2)}, u32[]{:S(2)}) collective-permute-start(f32[128,128]{1,0:T(8,128)S(1)} %add.252), channel_id=1, source_target_pairs={{0,1},{1,0},{2,3},{3,2},{4,5},{5,4},{6,7},{7,6},{8,9},{9,8},{10,11... | collective-permute-start | bytes 196616 | tf_op jit(solution)/shard_map/ppermute | solution.py:331
  33.7 1.2 pad_bitcast_fusion
  34.9 1.3 collective-permute-done.6
  36.2 2.8 %collective-permute-start.20 = (bf16[16,128]{1,0:T(8,128)(2,1)S(1)}, bf16[16,128]{1,0:T(8,128)(2,1)S(1)}, u32[]{:S(2)}, u32[]{:S(2)}) collective-permute-start(bf16[16,128]{1,0:T(8,128)(2,1)S(1)} %convert_bitcast_fusion), channel_id=1, source_target_pairs={{0,3},{1,0},{2,1},{3,2},{4,7},{5,4},{6,5},{7,6},{8,11},{9,8},{10,9... | collective-permute-start | bytes 12296 | tf_op jit(solution)/shard_map/ppermute | solution.py:323
  39.1 1.3 collective-permute-done.20
  40.4 1.1 collective-permute-start.7
  41.5 2.7 %constant_dynamic-slice_fusion.4 = (bf16[1024,128]{1,0:T(8,128)(2,1)}, bf16[1024,128]{1,0:T(8,128)(2,1)}, bf16[1024,128]{1,0:T(8,128)(2,1)}, bf16[1024,128]{1,0:...) fusion(bf16[8192,128]{1,0:T(8,128)(2,1)} %param.24, ...), kind=kLoop, calls=%fused_computation.71 | loop fusion | bytes 4194336 | tf_op jit(solution)/shard_map/dynamic_slice | solution.py:412
  44.3 3.6 %collective-permute-start = (bf16[1024,128]{1,0:T(8,128)(2,1)}, bf16[1024,128]{1,0:T(8,128)(2,1)}, u32[]{:S(2)}, u32[]{:S(2)}) collective-permute-start(bf16[1024,128]{1,0:T(8,128)(2,1)} %get-tuple-element.105), channel_id=1, source_target_pairs={{0,1},{1,2},{2,3},{3,0},{4,5},{5,6},{6,7},{7,4},{8,9},{9,10},{10,1... | collective-permute-start | bytes 786440 | tf_op jit(solution)/shard_map/ppermute | solution.py:323
  48.5 1.9 collective-permute-start.2
  52.4 1.0 copy.53
  56.3 2.6 %row_weights.1.weights_ref = f32[1,2048]{1,0:T(1,128)} custom-call(s32[1,2048]{1,0:T(1,128)} %bitcast.78, f32[128,128]{1,0:T(8,128)} %add.254.counts_ref), custom_call_target="tpu_custom_call" | custom-call | tf_op jit(solution)/shard_map/row_weights/pallas_call | solution.py:365
  59.0 2.3 collective-permute-start.22
  61.4 4.1 %prepare_first.1 = (bf16[512,2048]{1,0:T(8,128)(2,1)}, bf16[2048,512]{1,0:T(8,128)(2,1)}) custom-call(s32[1]{0:T(128)} %bitcast.place_ref, bf16[512,256]{1,0:T(8,128)(2,1)} %copy-done.5, bf16[512,256]{1,0:T(8,128)(2,1)} %copy-done.11, bf16[512,256]{1,0:T(8,128)(2,1)} %copy-done.8, bf16[512,256]{1,0:T(8,128)(2,1)} %copy-done.12, bf16[512,256]{1,0:T(8,128)(2,1)} %copy-done.9, ...), custom_call_target="tpu_custom_call" | custom-call | tf_op jit(solution)/shard_map/prepare_first/pallas_call | solution.py:374
  65.5 1.4 collective-permute-start.23
  66.8 0.8 broadcast_in_dim.10.bias_top_ref
  67.6 1.3 broadcast_in_dim.8.bias_one_ref
  69.0 1.0 broadcast_in_dim.9.bias_two_ref
  70.0 22.1 %layers.2 = (bf16[2064,1024]{1,0:T(8,128)(2,1)}, f32[2,1024]{1,0:T(2,128)}, f32[2064,512]{1,0:T(8,128)}, f32[2048,128]{1,0:T(8,128)}, f32[256,128]{1,0:T(8,128)}...) custom-call(s32[1]{0:T(128)} %bitcast.place_ref, bf16[1024,128]{1,0:T(8,128)(2,1)} %get-tuple-element.106.x0, ...), custom_call_target="tpu_custom_call" | custom-call | flops 8192000000 | bytes 20000000 | tf_op jit(solution)/shard_map/layers/pallas_call | solution.py:471
  92.9 25.2 %layers.3 = (bf16[2064,1024]{1,0:T(8,128)(2,1)}, f32[2,1024]{1,0:T(2,128)}, bf16[2,4,256,640]{3,2,1,0:T(8,128)(2,1)}, f32[16,512]{1,0:T(8,128)}, f32[160,128]{1,0:T(8,128)}) custom-call(s32[1]{0:T(128)} %bitcast.place_ref, bf16[1024,128]{1,0:T(8,128)(2,1)} %get-tuple-element.103.x0, bf16[1024,128]{1,0:T(8,128)(2,1)} %copy-done.35, ...), custom_call_target="tpu_custom_call" | custom-call | flops 8192000000 | bytes 20000000 | tf_op jit(solution)/shard_map/layers/pallas_call | solution.py:471
  118.2 0.9 constant_dynamic-update-slice_fusion.4
  121.9 1.4 slice_bitcast_fusion
  123.9 6.4 %input_gradients.2 = (f32[1024,128]{1,0:T(8,128)}, bf16[1024,128]{1,0:T(8,128)(2,1)}, bf16[1024,128]{1,0:T(8,128)(2,1)}, bf16[1024,128]{1,0:T(8,128)(2,1)}) custom-call(bf16[2064,1024]{1,0:T(8,128)(2,1)} %get-tuple-element.60.d_ref, bf16[512,2048]{1,0:T(8,128)(2,1)} %get-tuple-element.61.first_ref, bf16[512,16]{1,0:T(8,128)(2,1)} %bitcast.75), custom_call_target="tpu_custom_call" | custom-call | flops 2048000000 | bytes 8000000 | tf_op jit(solution)/shard_map/input_gradients/pallas_call | solution.py:493
  130.3 19.1 %collective-permute-start.24 = (bf16[1024,128]{1,0:T(8,128)(2,1)}, bf16[1024,128]{1,0:T(8,128)(2,1)S(1)}, u32[]{:S(2)}, u32[]{:S(2)}) collective-permute-start(bf16[1024,128]{1,0:T(8,128)(2,1)} %get-tuple-element.63), channel_id=1, source_target_pairs={{0,3},{1,0},{2,1},{3,2},{4,7},{5,4},{6,5},{7,6},{8,11},{9,8},{10,9... | collective-permute-start | bytes 786440 | tf_op jit(solution)/shard_map/ppermute | solution.py:323
  150.7 6.5 %input_gradients.3 = (f32[1024,128]{1,0:T(8,128)}, bf16[1024,128]{1,0:T(8,128)(2,1)}, bf16[1024,128]{1,0:T(8,128)(2,1)}, bf16[1024,128]{1,0:T(8,128)(2,1)}) custom-call(bf16[2064,1024]{1,0:T(8,128)(2,1)} %get-tuple-element.66.d_ref, bf16[512,2048]{1,0:T(8,128)(2,1)} %get-tuple-element.61.first_ref, bf16[512,16]{1,0:T(8,128)(2,1)} %bitcast.76), custom_call_target="tpu_custom_call" | custom-call | flops 2048000000 | bytes 8000000 | tf_op jit(solution)/shard_map/input_gradients/pallas_call | solution.py:493
  158.2 3.9 %collective-permute-done.45 = f32[224,128]{1,0:T(8,128)S(1)} collective-permute-done((f32[224,128]{1,0:T(8,128)S(1)}, f32[224,128]{1,0:T(8,128)S(1)}, u32[]{:S(2)}, u32[]{:S(2)}) %collective-permute-start.45) | collective-permute-done | bytes 114720 | tf_op jit(solution)/shard_map/ppermute | solution.py:326
  162.1 3.2 %collective-permute-start.27 = (bf16[1024,128]{1,0:T(8,128)(2,1)S(1)}, bf16[1024,128]{1,0:T(8,128)(2,1)S(1)}, u32[]{:S(2)}, u32[]{:S(2)}) collective-permute-start(bf16[1024,128]{1,0:T(8,128)(2,1)S(1)} %copy-done.37), channel_id=1, source_target_pairs={{0,3},{1,0},{2,1},{3,2},{4,7},{5,4},{6,5},{7,6},{8,11},{9,8},{10,9... | collective-permute-start | bytes 786440 | tf_op jit(solution)/shard_map/ppermute | solution.py:323
  165.3 1.2 collective-permute-start.28
  166.5 5.8 %collective-permute-done.25 = bf16[1024,128]{1,0:T(8,128)(2,1)S(1)} collective-permute-done((bf16[1024,128]{1,0:T(8,128)(2,1)}, bf16[1024,128]{1,0:T(8,128)(2,1)S(1)}, u32[]{:S(2)}, u32[]{:S(2)}) %collective-permute-start.25) | collective-permute-done | bytes 262176 | tf_op jit(solution)/shard_map/ppermute | solution.py:323
  172.9 4.0 %collective-permute-done.27 = bf16[1024,128]{1,0:T(8,128)(2,1)S(1)} collective-permute-done((bf16[1024,128]{1,0:T(8,128)(2,1)S(1)}, bf16[1024,128]{1,0:T(8,128)(2,1)S(1)}, u32[]{:S(2)}, u32[]{:S(2)}) %collective-permute-start.27) | collective-permute-done | bytes 262176 | tf_op jit(solution)/shard_map/ppermute | solution.py:323
  177.0 16.9 %collective-permute-done.28 = bf16[1024,128]{1,0:T(8,128)(2,1)S(1)} collective-permute-done((bf16[1024,128]{1,0:T(8,128)(2,1)S(1)}, bf16[1024,128]{1,0:T(8,128)(2,1)S(1)}, u32[]{:S(2)}, u32[]{:S(2)}) %collective-permute-start.28) | collective-permute-done | bytes 262176 | tf_op jit(solution)/shard_map/ppermute | solution.py:323
  194.0 1.5 collective-permute-start.50
  195.6 3.4 %collective-permute-start.47 = (f32[16,128]{1,0:T(8,128)S(1)}, f32[16,128]{1,0:T(8,128)S(1)}, u32[]{:S(2)}, u32[]{:S(2)}) collective-permute-start(f32[16,128]{1,0:T(8,128)S(1)} %get-tuple-element.116), channel_id=1, source_target_pairs={{0,3},{1,0},{2,1},{3,2},{4,7},{5,4},{6,5},{7,6},{8,11},{9,8},{10,9... | collective-permute-start | bytes 24584 | tf_op jit(solution)/shard_map/ppermute | solution.py:323
  199.6 2.4 collective-permute-start.51
  202.0 1.5 collective-permute-done.48
  203.5 1.0 collective-permute-done.49
  207.0 2.6 %collective-permute-start.33 = (bf16[256,640]{1,0:T(8,128)(2,1)S(1)}, bf16[256,640]{1,0:T(8,128)(2,1)S(1)}, u32[]{:S(2)}, u32[]{:S(2)}) collective-permute-start(bf16[256,640]{1,0:T(8,128)(2,1)S(1)} %get-tuple-element.110), channel_id=1, source_target_pairs={{0,24},{4,28},{8,16},{12,20},{16,8},{20,12},{24,0},{28,4},{1,25},{... | collective-permute-start | bytes 983048 | tf_op jit(solution)/shard_map/ppermute | solution.py:326
  210.3 6.0 %collective-permute-done.31 = bf16[256,640]{1,0:T(8,128)(2,1)S(1)} collective-permute-done((bf16[256,640]{1,0:T(8,128)(2,1)S(1)}, bf16[256,640]{1,0:T(8,128)(2,1)S(1)}, u32[]{:S(2)}, u32[]{:S(2)}) %collective-permute-start.31) | collective-permute-done | bytes 327712 | tf_op jit(solution)/shard_map/ppermute | solution.py:326
  216.4 3.8 %collective-permute-done.32 = bf16[256,640]{1,0:T(8,128)(2,1)S(1)} collective-permute-done((bf16[256,640]{1,0:T(8,128)(2,1)S(1)}, bf16[256,640]{1,0:T(8,128)(2,1)S(1)}, u32[]{:S(2)}, u32[]{:S(2)}) %collective-permute-start.32) | collective-permute-done | bytes 327712 | tf_op jit(solution)/shard_map/ppermute | solution.py:326
  220.4 3.9 %collective-permute-start.35 = (bf16[256,256]{1,0:T(8,128)(2,1)S(1)}, bf16[256,256]{1,0:T(8,128)(2,1)S(1)}, u32[]{:S(2)}, u32[]{:S(2)}) collective-permute-start(bf16[256,256]{1,0:T(8,128)(2,1)S(1)} %get-tuple-element.119), channel_id=1, source_target_pairs={{0,3},{1,0},{2,1},{3,2},{4,7},{5,4},{6,5},{7,6},{8,11},{9,8},{10,9... | collective-permute-start | bytes 393224 | tf_op jit(solution)/shard_map/ppermute | solution.py:323
  225.6 2.2 collective-permute-done.35
  227.8 4.2 %collective-permute-done.36 = bf16[256,256]{1,0:T(8,128)(2,1)S(1)} collective-permute-done((bf16[256,256]{1,0:T(8,128)(2,1)S(1)}, bf16[256,256]{1,0:T(8,128)(2,1)S(1)}, u32[]{:S(2)}, u32[]{:S(2)}) %collective-permute-start.36) | collective-permute-done | bytes 131104 | tf_op jit(solution)/shard_map/ppermute | solution.py:323
  232.2 1.1 collective-permute-start.38
  233.3 1.1 collective-permute-start.40
  234.4 1.3 collective-permute-start.42
  236.3 2.3 collective-permute-done.38
  238.6 1.8 collective-permute-done.40
  240.4 1.6 collective-permute-done.42
  242.1 1.2 collective-permute-done.43
  243.4 1.0 copy-done.4
  244.3 9.0 %update_layers.1 = (f32[128,2048]{1,0:T(8,128)}, f32[128,2048]{1,0:T(8,128)}, f32[128,2048]{1,0:T(8,128)}, f32[2048,128]{1,0:T(8,128)}, f32[2048,128]{1,0:T(8,12...) custom-call(s32[1]{0:T(128)} %bitcast.place_ref, bf16[8,256,256]{2,1,0:T(8,128)(2,1)} %copy-done.4, f32[128,2048]{1,0:T(8,128)} %first_w.1, ...), custom_call_target="tpu_custom_call" | custom-call | flops 1000000 | bytes 15000000 | tf_op jit(solution)/shard_map/update_layers/pallas_call | solution.py:554
  (196 shorter events, 21.9 us)
Async XLA Ops:
  0.7 51.7 %copy-start = (f32[2048,128]{1,0:T(8,128)S(1)}, f32[2048,128]{1,0:T(8,128)}, u32[]{:S(2)}) copy-start(f32[2048,128]{1,0:T(8,128)} %second_w.1) | copy-start | bytes 3145732
  1.7 7.8 %collective-permute-start.10 = (bf16[128,256]{1,0:T(8,128)(2,1)S(1)}, bf16[128,256]{1,0:T(8,128)(2,1)S(1)}, u32[]{:S(2)}, u32[]{:S(2)}) collective-permute-start(bf16[128,256]{1,0:T(8,128)(2,1)S(1)} %dynamic-slice_convert_fusion), channel_id=1, source_target_pairs={{0,3},{1,0},{2,1},{3,2},{4,7},{5,4},{6,5},{7,6},{8,11},{9,8},{10,9... | collective-permute-start | bytes 196616 | tf_op jit(solution)/shard_map/ppermute | solution.py:323
  6.8 6.2 %collective-permute-start.8 = (bf16[128,256]{1,0:T(8,128)(2,1)S(1)}, bf16[128,256]{1,0:T(8,128)(2,1)S(1)}, u32[]{:S(2)}, u32[]{:S(2)}) collective-permute-start(bf16[128,256]{1,0:T(8,128)(2,1)S(1)} %dynamic-slice_convert_fusion), channel_id=1, source_target_pairs={{0,1},{1,2},{2,3},{3,0},{4,5},{5,6},{6,7},{7,4},{8,9},{9,10},{10,1... | collective-permute-start | bytes 196616 | tf_op jit(solution)/shard_map/ppermute | solution.py:323
  6.8 7.5 %collective-permute-start.9 = (bf16[128,256]{1,0:T(8,128)(2,1)S(1)}, bf16[128,256]{1,0:T(8,128)(2,1)S(1)}, u32[]{:S(2)}, u32[]{:S(2)}) collective-permute-start(bf16[128,256]{1,0:T(8,128)(2,1)S(1)} %dynamic-slice_convert_fusion), channel_id=1, source_target_pairs={{0,2},{1,3},{2,0},{3,1},{4,6},{5,7},{6,4},{7,5},{8,10},{9,11},{10,... | collective-permute-start | bytes 196616 | tf_op jit(solution)/shard_map/ppermute | solution.py:323
  9.5 6.4 %collective-permute-start.3 = (f32[128,128]{1,0:T(8,128)}, f32[128,128]{1,0:T(8,128)S(1)}, u32[]{:S(2)}, u32[]{:S(2)}) collective-permute-start(f32[128,128]{1,0:T(8,128)} %user_counts.1), channel_id=1, source_target_pairs={{0,4},{4,0},{8,12},{12,8},{16,20},{20,16},{24,28},{28,24},{1,5},{5... | collective-permute-start | bytes 196616 | tf_op jit(solution)/shard_map/ppermute | solution.py:326
  14.3 40.6 %copy-start.5 = (bf16[512,256]{1,0:T(8,128)(2,1)}, bf16[512,256]{1,0:T(8,128)(2,1)S(1)}, u32[]{:S(2)}) copy-start(bf16[512,256]{1,0:T(8,128)(2,1)S(1)} %pad_maximum_fusion.refs_0_) | copy-start | bytes 786436
  14.3 19.3 %collective-permute-start.12 = (bf16[512,256]{1,0:T(8,128)(2,1)S(1)}, bf16[512,256]{1,0:T(8,128)(2,1)S(1)}, u32[]{:S(2)}, u32[]{:S(2)}) collective-permute-start(bf16[512,256]{1,0:T(8,128)(2,1)S(1)} %pad_maximum_fusion.refs_0_), channel_id=1, source_target_pairs={{0,8},{4,12},{8,0},{12,4},{16,24},{20,28},{24,16},{28,20},{1,9},{5... | collective-permute-start | bytes 786440 | tf_op jit(solution)/shard_map/ppermute | solution.py:326
  16.7 4.7 %collective-permute-start.4 = (f32[128,128]{1,0:T(8,128)S(1)}, f32[128,128]{1,0:T(8,128)S(1)}, u32[]{:S(2)}, u32[]{:S(2)}) collective-permute-start(f32[128,128]{1,0:T(8,128)S(1)} %add.250), channel_id=1, source_target_pairs={{0,8},{4,12},{8,0},{12,4},{16,24},{20,28},{24,16},{28,20},{1,9},{5... | collective-permute-start | bytes 196616 | tf_op jit(solution)/shard_map/ppermute | solution.py:326
  18.0 12.8 %collective-permute-start.18 = (bf16[16,128]{1,0:T(8,128)(2,1)S(1)}, bf16[16,128]{1,0:T(8,128)(2,1)S(1)}, u32[]{:S(2)}, u32[]{:S(2)}) collective-permute-start(bf16[16,128]{1,0:T(8,128)(2,1)S(1)} %convert_bitcast_fusion), channel_id=1, source_target_pairs={{0,1},{1,2},{2,3},{3,0},{4,5},{5,6},{6,7},{7,4},{8,9},{9,10},{10,1... | collective-permute-start | bytes 12296 | tf_op jit(solution)/shard_map/ppermute | solution.py:323
  18.0 12.9 %collective-permute-start.19 = (bf16[16,128]{1,0:T(8,128)(2,1)S(1)}, bf16[16,128]{1,0:T(8,128)(2,1)S(1)}, u32[]{:S(2)}, u32[]{:S(2)}) collective-permute-start(bf16[16,128]{1,0:T(8,128)(2,1)S(1)} %convert_bitcast_fusion), channel_id=1, source_target_pairs={{0,2},{1,3},{2,0},{3,1},{4,6},{5,7},{6,4},{7,5},{8,10},{9,11},{10,... | collective-permute-start | bytes 12296 | tf_op jit(solution)/shard_map/ppermute | solution.py:323
  21.4 7.5 %collective-permute-start.5 = (f32[128,128]{1,0:T(8,128)S(1)}, f32[128,128]{1,0:T(8,128)S(1)}, u32[]{:S(2)}, u32[]{:S(2)}) collective-permute-start(f32[128,128]{1,0:T(8,128)S(1)} %add.251), channel_id=1, source_target_pairs={{0,16},{4,20},{8,24},{12,28},{16,0},{20,4},{24,8},{28,12},{1,17},{... | collective-permute-start | bytes 196616 | tf_op jit(solution)/shard_map/ppermute | solution.py:326
  24.6 19.7 %collective-permute-start.14 = (bf16[512,256]{1,0:T(8,128)(2,1)S(1)}, bf16[512,256]{1,0:T(8,128)(2,1)S(1)}, u32[]{:S(2)}, u32[]{:S(2)}) collective-permute-start(bf16[512,256]{1,0:T(8,128)(2,1)S(1)} %pad_maximum_fusion.refs_0_), channel_id=1, source_target_pairs={{0,16},{4,20},{8,24},{12,28},{16,0},{20,4},{24,8},{28,12},{1,17},{... | collective-permute-start | bytes 786440 | tf_op jit(solution)/shard_map/ppermute | solution.py:326
  28.9 19.0 %collective-permute-start.16 = (bf16[512,256]{1,0:T(8,128)(2,1)S(1)}, bf16[512,256]{1,0:T(8,128)(2,1)S(1)}, u32[]{:S(2)}, u32[]{:S(2)}) collective-permute-start(bf16[512,256]{1,0:T(8,128)(2,1)S(1)} %pad_maximum_fusion.refs_0_), channel_id=1, source_target_pairs={{0,24},{4,28},{8,16},{12,20},{16,8},{20,12},{24,0},{28,4},{1,25},{... | collective-permute-start | bytes 786440 | tf_op jit(solution)/shard_map/ppermute | solution.py:326
  30.8 17.7 %collective-permute-start.11 = (bf16[512,256]{1,0:T(8,128)(2,1)S(1)}, bf16[512,256]{1,0:T(8,128)(2,1)S(1)}, u32[]{:S(2)}, u32[]{:S(2)}) collective-permute-start(bf16[512,256]{1,0:T(8,128)(2,1)S(1)} %pad_maximum_fusion.refs_0_), channel_id=1, source_target_pairs={{0,4},{4,0},{8,12},{12,8},{16,20},{20,16},{24,28},{28,24},{1,5},{5... | collective-permute-start | bytes 786440 | tf_op jit(solution)/shard_map/ppermute | solution.py:326
  30.9 5.4 %collective-permute-start.6 = (f32[128,128]{1,0:T(8,128)S(1)}, f32[128,128]{1,0:T(8,128)S(1)}, u32[]{:S(2)}, u32[]{:S(2)}) collective-permute-start(f32[128,128]{1,0:T(8,128)S(1)} %add.252), channel_id=1, source_target_pairs={{0,1},{1,0},{2,3},{3,2},{4,5},{5,4},{6,7},{7,6},{8,9},{9,8},{10,11... | collective-permute-start | bytes 196616 | tf_op jit(solution)/shard_map/ppermute | solution.py:331
  33.6 27.8 %copy-start.8 = (bf16[512,256]{1,0:T(8,128)(2,1)}, bf16[512,256]{1,0:T(8,128)(2,1)S(1)}, u32[]{:S(2)}) copy-start(bf16[512,256]{1,0:T(8,128)(2,1)S(1)} %collective-permute-done.12.refs_2_) | copy-start | bytes 786436
  33.6 16.8 %collective-permute-start.13 = (bf16[512,256]{1,0:T(8,128)(2,1)S(1)}, bf16[512,256]{1,0:T(8,128)(2,1)S(1)}, u32[]{:S(2)}, u32[]{:S(2)}) collective-permute-start(bf16[512,256]{1,0:T(8,128)(2,1)S(1)} %collective-permute-done.12.refs_2_), channel_id=1, source_target_pairs={{0,4},{4,0},{8,12},{12,8},{16,20},{20,16},{24,28},{28,24},{1,5},{5... | collective-permute-start | bytes 786440 | tf_op jit(solution)/shard_map/ppermute | solution.py:326
  36.2 4.1 %collective-permute-start.20 = (bf16[16,128]{1,0:T(8,128)(2,1)S(1)}, bf16[16,128]{1,0:T(8,128)(2,1)S(1)}, u32[]{:S(2)}, u32[]{:S(2)}) collective-permute-start(bf16[16,128]{1,0:T(8,128)(2,1)S(1)} %convert_bitcast_fusion), channel_id=1, source_target_pairs={{0,3},{1,0},{2,1},{3,2},{4,7},{5,4},{6,5},{7,6},{8,11},{9,8},{10,9... | collective-permute-start | bytes 12296 | tf_op jit(solution)/shard_map/ppermute | solution.py:323
  39.1 28.6 %slice-start = ((f32[3202]{0:T(1024)}), f32[2048]{0:T(1024)S(1)}, s32[]{:S(2)}) async-start(f32[3202]{0:T(1024)} %param.42), calls=%async_computation | async-start | bytes 16384 | tf_op jit(solution)/shard_map/slice | solution.py:398
  40.4 10.0 %collective-permute-start.7 = (f32[128,128]{1,0:T(8,128)S(1)}, f32[128,128]{1,0:T(8,128)S(1)}, u32[]{:S(2)}, u32[]{:S(2)}) collective-permute-start(f32[128,128]{1,0:T(8,128)S(1)} %add.253), channel_id=1, source_target_pairs={{0,2},{1,3},{2,0},{3,1},{4,6},{5,7},{6,4},{7,5},{8,10},{9,11},{10,... | collective-permute-start | bytes 196616 | tf_op jit(solution)/shard_map/ppermute | solution.py:331
  44.3 21.2 %collective-permute-start = (bf16[1024,128]{1,0:T(8,128)(2,1)}, bf16[1024,128]{1,0:T(8,128)(2,1)}, u32[]{:S(2)}, u32[]{:S(2)}) collective-permute-start(bf16[1024,128]{1,0:T(8,128)(2,1)} %get-tuple-element.105), channel_id=1, source_target_pairs={{0,1},{1,2},{2,3},{3,0},{4,5},{5,6},{6,7},{7,4},{8,9},{9,10},{10,1... | collective-permute-start | bytes 786440 | tf_op jit(solution)/shard_map/ppermute | solution.py:323
  47.9 18.9 %collective-permute-start.1 = (bf16[1024,128]{1,0:T(8,128)(2,1)}, bf16[1024,128]{1,0:T(8,128)(2,1)}, u32[]{:S(2)}, u32[]{:S(2)}) collective-permute-start(bf16[1024,128]{1,0:T(8,128)(2,1)} %get-tuple-element.104), channel_id=1, source_target_pairs={{0,2},{1,3},{2,0},{3,1},{4,6},{5,7},{6,4},{7,5},{8,10},{9,11},{10,... | collective-permute-start | bytes 786440 | tf_op jit(solution)/shard_map/ppermute | solution.py:323
  48.5 18.3 %collective-permute-start.2 = (bf16[1024,128]{1,0:T(8,128)(2,1)}, bf16[1024,128]{1,0:T(8,128)(2,1)}, u32[]{:S(2)}, u32[]{:S(2)}) collective-permute-start(bf16[1024,128]{1,0:T(8,128)(2,1)} %get-tuple-element.101), channel_id=1, source_target_pairs={{0,3},{1,0},{2,1},{3,2},{4,7},{5,4},{6,5},{7,6},{8,11},{9,8},{10,9... | collective-permute-start | bytes 786440 | tf_op jit(solution)/shard_map/ppermute | solution.py:323
  50.4 8.5 %collective-permute-start.15 = (bf16[512,256]{1,0:T(8,128)(2,1)S(1)}, bf16[512,256]{1,0:T(8,128)(2,1)}, u32[]{:S(2)}, u32[]{:S(2)}) collective-permute-start(bf16[512,256]{1,0:T(8,128)(2,1)S(1)} %collective-permute-done.14.refs_4_), channel_id=1, source_target_pairs={{0,4},{4,0},{8,12},{12,8},{16,20},{20,16},{24,28},{28,24},{1,5},{5... | collective-permute-start | bytes 786440 | tf_op jit(solution)/shard_map/ppermute | solution.py:326
  50.4 8.6 %collective-permute-start.17 = (bf16[512,256]{1,0:T(8,128)(2,1)S(1)}, bf16[512,256]{1,0:T(8,128)(2,1)}, u32[]{:S(2)}, u32[]{:S(2)}) collective-permute-start(bf16[512,256]{1,0:T(8,128)(2,1)S(1)} %collective-permute-done.16.refs_6_), channel_id=1, source_target_pairs={{0,4},{4,0},{8,12},{12,8},{16,20},{20,16},{24,28},{28,24},{1,5},{5... | collective-permute-start | bytes 786440 | tf_op jit(solution)/shard_map/ppermute | solution.py:326
  58.9 33.2 %collective-permute-start.21 = (bf16[1024,128]{1,0:T(8,128)(2,1)}, bf16[1024,128]{1,0:T(8,128)(2,1)S(1)}, u32[]{:S(2)}, u32[]{:S(2)}) collective-permute-start(bf16[1024,128]{1,0:T(8,128)(2,1)} %get-tuple-element.102), channel_id=1, source_target_pairs={{0,1},{1,2},{2,3},{3,0},{4,5},{5,6},{6,7},{7,4},{8,9},{9,10},{10,1... | collective-permute-start | bytes 786440 | tf_op jit(solution)/shard_map/ppermute | solution.py:323
  59.0 33.0 %collective-permute-start.22 = (bf16[1024,128]{1,0:T(8,128)(2,1)}, bf16[1024,128]{1,0:T(8,128)(2,1)S(1)}, u32[]{:S(2)}, u32[]{:S(2)}) collective-permute-start(bf16[1024,128]{1,0:T(8,128)(2,1)} %get-tuple-element.108), channel_id=1, source_target_pairs={{0,2},{1,3},{2,0},{3,1},{4,6},{5,7},{6,4},{7,5},{8,10},{9,11},{10,... | collective-permute-start | bytes 786440 | tf_op jit(solution)/shard_map/ppermute | solution.py:323
  65.5 26.6 %collective-permute-start.23 = (bf16[1024,128]{1,0:T(8,128)(2,1)S(1)}, bf16[1024,128]{1,0:T(8,128)(2,1)S(1)}, u32[]{:S(2)}, u32[]{:S(2)}) collective-permute-start(bf16[1024,128]{1,0:T(8,128)(2,1)S(1)} %get-tuple-element.107), channel_id=1, source_target_pairs={{0,3},{1,0},{2,1},{3,2},{4,7},{5,4},{6,5},{7,6},{8,11},{9,8},{10,9... | collective-permute-start | bytes 786440 | tf_op jit(solution)/shard_map/ppermute | solution.py:323
  121.9 35.3 %collective-permute-start.44 = (f32[224,128]{1,0:T(8,128)S(1)}, f32[224,128]{1,0:T(8,128)S(1)}, u32[]{:S(2)}, u32[]{:S(2)}) collective-permute-start(f32[224,128]{1,0:T(8,128)S(1)} %constant_dynamic-update-slice_fusion), channel_id=1, source_target_pairs={{0,4},{4,0},{8,12},{12,8},{16,20},{20,16},{24,28},{28,24},{1,5},{5... | collective-permute-start | bytes 344072 | tf_op jit(solution)/shard_map/ppermute | solution.py:326
  123.3 82.1 %collective-permute-start.30 = (bf16[4,256,640]{2,1,0:T(8,128)(2,1)S(1)}, bf16[4,256,640]{2,1,0:T(8,128)(2,1)S(1)}, u32[]{:S(2)}, u32[]{:S(2)}) collective-permute-start(bf16[4,256,640]{2,1,0:T(8,128)(2,1)S(1)} %slice_bitcast_fusion), channel_id=1, source_target_pairs={{0,4},{4,0},{8,12},{12,8},{16,20},{20,16},{24,28},{28,24},{1,5},{5... | collective-permute-start | bytes 3932168 | tf_op jit(solution)/shard_map/ppermute | solution.py:326
  130.3 34.9 %collective-permute-start.24 = (bf16[1024,128]{1,0:T(8,128)(2,1)}, bf16[1024,128]{1,0:T(8,128)(2,1)S(1)}, u32[]{:S(2)}, u32[]{:S(2)}) collective-permute-start(bf16[1024,128]{1,0:T(8,128)(2,1)} %get-tuple-element.63), channel_id=1, source_target_pairs={{0,3},{1,0},{2,1},{3,2},{4,7},{5,4},{6,5},{7,6},{8,11},{9,8},{10,9... | collective-permute-start | bytes 786440 | tf_op jit(solution)/shard_map/ppermute | solution.py:323
  149.4 22.9 %collective-permute-start.25 = (bf16[1024,128]{1,0:T(8,128)(2,1)}, bf16[1024,128]{1,0:T(8,128)(2,1)S(1)}, u32[]{:S(2)}, u32[]{:S(2)}) collective-permute-start(bf16[1024,128]{1,0:T(8,128)(2,1)} %get-tuple-element.64), channel_id=1, source_target_pairs={{0,2},{1,3},{2,0},{3,1},{4,6},{5,7},{6,4},{7,5},{8,10},{9,11},{10,... | collective-permute-start | bytes 786440 | tf_op jit(solution)/shard_map/ppermute | solution.py:323
  149.4 22.9 %collective-permute-start.26 = (bf16[1024,128]{1,0:T(8,128)(2,1)}, bf16[1024,128]{1,0:T(8,128)(2,1)S(1)}, u32[]{:S(2)}, u32[]{:S(2)}) collective-permute-start(bf16[1024,128]{1,0:T(8,128)(2,1)} %get-tuple-element.65), channel_id=1, source_target_pairs={{0,1},{1,2},{2,3},{3,0},{4,5},{5,6},{6,7},{7,4},{8,9},{9,10},{10,1... | collective-permute-start | bytes 786440 | tf_op jit(solution)/shard_map/ppermute | solution.py:323
  157.2 4.9 %collective-permute-start.45 = (f32[224,128]{1,0:T(8,128)S(1)}, f32[224,128]{1,0:T(8,128)S(1)}, u32[]{:S(2)}, u32[]{:S(2)}) collective-permute-start(f32[224,128]{1,0:T(8,128)S(1)} %add.272), channel_id=1, source_target_pairs={{0,8},{4,12},{8,0},{12,4},{16,24},{20,28},{24,16},{28,20},{1,9},{5... | collective-permute-start | bytes 344072 | tf_op jit(solution)/shard_map/ppermute | solution.py:326
  158.1 46.4 %copy-start.19 = (f32[128,16]{0,1:T(8,128)S(1)}, f32[128,16]{0,1:T(8,128)}, u32[]{:S(2)}) copy-start(f32[128,16]{0,1:T(8,128)} %param.30) | copy-start | bytes 24580
  158.1 46.4 %copy-start.22 = (f32[128,16]{0,1:T(8,128)S(1)}, f32[128,16]{0,1:T(8,128)}, u32[]{:S(2)}) copy-start(f32[128,16]{0,1:T(8,128)} %param.31) | copy-start | bytes 24580
  158.1 46.4 %copy-start.23 = (f32[128,16]{0,1:T(8,128)S(1)}, f32[128,16]{0,1:T(8,128)}, u32[]{:S(2)}) copy-start(f32[128,16]{0,1:T(8,128)} %param.32) | copy-start | bytes 24580
  158.2 47.3 %copy-start.2 = (bf16[2,4,256,640]{3,2,1,0:T(8,128)(2,1)S(1)}, bf16[2,4,256,640]{3,2,1,0:T(8,128)(2,1)}, u32[]{:S(2)}) copy-start(bf16[2,4,256,640]{3,2,1,0:T(8,128)(2,1)} %get-tuple-element.71) | copy-start | bytes 7864324
  162.1 14.9 %collective-permute-start.27 = (bf16[1024,128]{1,0:T(8,128)(2,1)S(1)}, bf16[1024,128]{1,0:T(8,128)(2,1)S(1)}, u32[]{:S(2)}, u32[]{:S(2)}) collective-permute-start(bf16[1024,128]{1,0:T(8,128)(2,1)S(1)} %copy-done.37), channel_id=1, source_target_pairs={{0,3},{1,0},{2,1},{3,2},{4,7},{5,4},{6,5},{7,6},{8,11},{9,8},{10,9... | collective-permute-start | bytes 786440 | tf_op jit(solution)/shard_map/ppermute | solution.py:323
  165.3 28.6 %collective-permute-start.28 = (bf16[1024,128]{1,0:T(8,128)(2,1)S(1)}, bf16[1024,128]{1,0:T(8,128)(2,1)S(1)}, u32[]{:S(2)}, u32[]{:S(2)}) collective-permute-start(bf16[1024,128]{1,0:T(8,128)(2,1)S(1)} %copy-done.34), channel_id=1, source_target_pairs={{0,2},{1,3},{2,0},{3,1},{4,6},{5,7},{6,4},{7,5},{8,10},{9,11},{10,... | collective-permute-start | bytes 786440 | tf_op jit(solution)/shard_map/ppermute | solution.py:323
  172.3 21.6 %collective-permute-start.29 = (bf16[1024,128]{1,0:T(8,128)(2,1)S(1)}, bf16[1024,128]{1,0:T(8,128)(2,1)S(1)}, u32[]{:S(2)}, u32[]{:S(2)}) collective-permute-start(bf16[1024,128]{1,0:T(8,128)(2,1)S(1)} %copy-done.33), channel_id=1, source_target_pairs={{0,1},{1,2},{2,3},{3,0},{4,5},{5,6},{6,7},{7,4},{8,9},{9,10},{10,1... | collective-permute-start | bytes 786440 | tf_op jit(solution)/shard_map/ppermute | solution.py:323
  172.4 21.6 %collective-permute-start.46 = (f32[224,128]{1,0:T(8,128)S(1)}, f32[224,128]{1,0:T(8,128)S(1)}, u32[]{:S(2)}, u32[]{:S(2)}) collective-permute-start(f32[224,128]{1,0:T(8,128)S(1)} %add.273), channel_id=1, source_target_pairs={{0,16},{4,20},{8,24},{12,28},{16,0},{20,4},{24,8},{28,12},{1,17},{... | collective-permute-start | bytes 344072 | tf_op jit(solution)/shard_map/ppermute | solution.py:326
  194.0 5.6 %collective-permute-start.50 = (f32[160,128]{1,0:T(8,128)S(1)}, f32[160,128]{1,0:T(8,128)S(1)}, u32[]{:S(2)}, u32[]{:S(2)}) collective-permute-start(f32[160,128]{1,0:T(8,128)S(1)} %slice.137), channel_id=1, source_target_pairs={{0,1},{1,0},{2,3},{3,2},{4,5},{5,4},{6,7},{7,6},{8,9},{9,8},{10,11... | collective-permute-start | bytes 245768 | tf_op jit(solution)/shard_map/ppermute | solution.py:331
  195.6 6.4 %collective-permute-start.47 = (f32[16,128]{1,0:T(8,128)S(1)}, f32[16,128]{1,0:T(8,128)S(1)}, u32[]{:S(2)}, u32[]{:S(2)}) collective-permute-start(f32[16,128]{1,0:T(8,128)S(1)} %get-tuple-element.116), channel_id=1, source_target_pairs={{0,3},{1,0},{2,1},{3,2},{4,7},{5,4},{6,5},{7,6},{8,11},{9,8},{10,9... | collective-permute-start | bytes 24584 | tf_op jit(solution)/shard_map/ppermute | solution.py:323
  199.0 4.5 %collective-permute-start.48 = (f32[16,128]{1,0:T(8,128)S(1)}, f32[16,128]{1,0:T(8,128)S(1)}, u32[]{:S(2)}, u32[]{:S(2)}) collective-permute-start(f32[16,128]{1,0:T(8,128)S(1)} %get-tuple-element.118), channel_id=1, source_target_pairs={{0,2},{1,3},{2,0},{3,1},{4,6},{5,7},{6,4},{7,5},{8,10},{9,11},{10,... | collective-permute-start | bytes 24584 | tf_op jit(solution)/shard_map/ppermute | solution.py:323
  199.0 5.5 %collective-permute-start.49 = (f32[16,128]{1,0:T(8,128)S(1)}, f32[16,128]{1,0:T(8,128)S(1)}, u32[]{:S(2)}, u32[]{:S(2)}) collective-permute-start(f32[16,128]{1,0:T(8,128)S(1)} %get-tuple-element.117), channel_id=1, source_target_pairs={{0,1},{1,2},{2,3},{3,0},{4,5},{5,6},{6,7},{7,4},{8,9},{9,10},{10,1... | collective-permute-start | bytes 24584 | tf_op jit(solution)/shard_map/ppermute | solution.py:323
  199.6 5.8 %collective-permute-start.51 = (f32[160,128]{1,0:T(8,128)S(1)}, f32[160,128]{1,0:T(8,128)S(1)}, u32[]{:S(2)}, u32[]{:S(2)}) collective-permute-start(f32[160,128]{1,0:T(8,128)S(1)} %slice_add_fusion.1), channel_id=1, source_target_pairs={{0,2},{1,3},{2,0},{3,1},{4,6},{5,7},{6,4},{7,5},{8,10},{9,11},{10,... | collective-permute-start | bytes 245768 | tf_op jit(solution)/shard_map/ppermute | solution.py:331
  205.9 29.9 %copy-start.29 = (f32[128]{0:T(128)S(1)}, f32[128]{0:T(128)}, u32[]{:S(2)}) copy-start(f32[128]{0:T(128)} %param.39) | copy-start | bytes 1540
  205.9 29.9 %copy-start.30 = (f32[128]{0:T(128)S(1)}, f32[128]{0:T(128)}, u32[]{:S(2)}) copy-start(f32[128]{0:T(128)} %param.47) | copy-start | bytes 1540
  205.9 29.9 %copy-start.31 = (f32[128]{0:T(128)S(1)}, f32[128]{0:T(128)}, u32[]{:S(2)}) copy-start(f32[128]{0:T(128)} %param.40) | copy-start | bytes 1540
  205.9 29.9 %copy-start.32 = (f32[128]{0:T(128)S(1)}, f32[128]{0:T(128)}, u32[]{:S(2)}) copy-start(f32[128]{0:T(128)} %param.41) | copy-start | bytes 1540
  206.0 10.4 %collective-permute-start.31 = (bf16[256,640]{1,0:T(8,128)(2,1)S(1)}, bf16[256,640]{1,0:T(8,128)(2,1)S(1)}, u32[]{:S(2)}, u32[]{:S(2)}) collective-permute-start(bf16[256,640]{1,0:T(8,128)(2,1)S(1)} %get-tuple-element.109), channel_id=1, source_target_pairs={{0,8},{4,12},{8,0},{12,4},{16,24},{20,28},{24,16},{28,20},{1,9},{5... | collective-permute-start | bytes 983048 | tf_op jit(solution)/shard_map/ppermute | solution.py:326
  206.6 13.5 %collective-permute-start.32 = (bf16[256,640]{1,0:T(8,128)(2,1)S(1)}, bf16[256,640]{1,0:T(8,128)(2,1)S(1)}, u32[]{:S(2)}, u32[]{:S(2)}) collective-permute-start(bf16[256,640]{1,0:T(8,128)(2,1)S(1)} %get-tuple-element.111), channel_id=1, source_target_pairs={{0,16},{4,20},{8,24},{12,28},{16,0},{20,4},{24,8},{28,12},{1,17},{... | collective-permute-start | bytes 983048 | tf_op jit(solution)/shard_map/ppermute | solution.py:326
  207.0 13.1 %collective-permute-start.33 = (bf16[256,640]{1,0:T(8,128)(2,1)S(1)}, bf16[256,640]{1,0:T(8,128)(2,1)S(1)}, u32[]{:S(2)}, u32[]{:S(2)}) collective-permute-start(bf16[256,640]{1,0:T(8,128)(2,1)S(1)} %get-tuple-element.110), channel_id=1, source_target_pairs={{0,24},{4,28},{8,16},{12,20},{16,8},{20,12},{24,0},{28,4},{1,25},{... | collective-permute-start | bytes 983048 | tf_op jit(solution)/shard_map/ppermute | solution.py:326
  220.4 7.4 %collective-permute-start.35 = (bf16[256,256]{1,0:T(8,128)(2,1)S(1)}, bf16[256,256]{1,0:T(8,128)(2,1)S(1)}, u32[]{:S(2)}, u32[]{:S(2)}) collective-permute-start(bf16[256,256]{1,0:T(8,128)(2,1)S(1)} %get-tuple-element.119), channel_id=1, source_target_pairs={{0,3},{1,0},{2,1},{3,2},{4,7},{5,4},{6,5},{7,6},{8,11},{9,8},{10,9... | collective-permute-start | bytes 393224 | tf_op jit(solution)/shard_map/ppermute | solution.py:323
  224.3 7.7 %collective-permute-start.36 = (bf16[256,256]{1,0:T(8,128)(2,1)S(1)}, bf16[256,256]{1,0:T(8,128)(2,1)S(1)}, u32[]{:S(2)}, u32[]{:S(2)}) collective-permute-start(bf16[256,256]{1,0:T(8,128)(2,1)S(1)} %get-tuple-element.120), channel_id=1, source_target_pairs={{0,2},{1,3},{2,0},{3,1},{4,6},{5,7},{6,4},{7,5},{8,10},{9,11},{10,... | collective-permute-start | bytes 393224 | tf_op jit(solution)/shard_map/ppermute | solution.py:323
  224.3 7.7 %collective-permute-start.34 = (bf16[256,256]{1,0:T(8,128)(2,1)S(1)}, bf16[256,256]{1,0:T(8,128)(2,1)S(1)}, u32[]{:S(2)}, u32[]{:S(2)}) collective-permute-start(bf16[256,256]{1,0:T(8,128)(2,1)S(1)} %concatenate.48), channel_id=1, source_target_pairs={{0,1},{1,2},{2,3},{3,0},{4,5},{5,6},{6,7},{7,4},{8,9},{9,10},{10,1... | collective-permute-start | bytes 393224 | tf_op jit(solution)/shard_map/ppermute | solution.py:323
  232.1 9.9 %collective-permute-start.37 = (bf16[256,256]{1,0:T(8,128)(2,1)S(1)}, bf16[256,256]{1,0:T(8,128)(2,1)S(1)}, u32[]{:S(2)}, u32[]{:S(2)}) collective-permute-start(bf16[256,256]{1,0:T(8,128)(2,1)S(1)} %get-tuple-element.96), channel_id=1, source_target_pairs={{0,4},{4,0},{8,12},{12,8},{16,20},{20,16},{24,28},{28,24},{1,5},{5... | collective-permute-start | bytes 393224 | tf_op jit(solution)/shard_map/ppermute | solution.py:326
  232.2 6.4 %collective-permute-start.38 = (bf16[256,256]{1,0:T(8,128)(2,1)S(1)}, bf16[256,256]{1,0:T(8,128)(2,1)S(1)}, u32[]{:S(2)}, u32[]{:S(2)}) collective-permute-start(bf16[256,256]{1,0:T(8,128)(2,1)S(1)} %get-tuple-element.96), channel_id=1, source_target_pairs={{0,8},{4,12},{8,0},{12,4},{16,24},{20,28},{24,16},{28,20},{1,9},{5... | collective-permute-start | bytes 393224 | tf_op jit(solution)/shard_map/ppermute | solution.py:326
  233.3 7.1 %collective-permute-start.40 = (bf16[256,256]{1,0:T(8,128)(2,1)S(1)}, bf16[256,256]{1,0:T(8,128)(2,1)S(1)}, u32[]{:S(2)}, u32[]{:S(2)}) collective-permute-start(bf16[256,256]{1,0:T(8,128)(2,1)S(1)} %get-tuple-element.96), channel_id=1, source_target_pairs={{0,16},{4,20},{8,24},{12,28},{16,0},{20,4},{24,8},{28,12},{1,17},{... | collective-permute-start | bytes 393224 | tf_op jit(solution)/shard_map/ppermute | solution.py:326
  234.4 7.6 %collective-permute-start.42 = (bf16[256,256]{1,0:T(8,128)(2,1)S(1)}, bf16[256,256]{1,0:T(8,128)(2,1)S(1)}, u32[]{:S(2)}, u32[]{:S(2)}) collective-permute-start(bf16[256,256]{1,0:T(8,128)(2,1)S(1)} %get-tuple-element.96), channel_id=1, source_target_pairs={{0,24},{4,28},{8,16},{12,20},{16,8},{20,12},{24,0},{28,4},{1,25},{... | collective-permute-start | bytes 393224 | tf_op jit(solution)/shard_map/ppermute | solution.py:326
  238.6 3.5 %collective-permute-start.39 = (bf16[256,256]{1,0:T(8,128)(2,1)S(1)}, bf16[256,256]{1,0:T(8,128)(2,1)S(1)}, u32[]{:S(2)}, u32[]{:S(2)}) collective-permute-start(bf16[256,256]{1,0:T(8,128)(2,1)S(1)} %collective-permute-done.38), channel_id=1, source_target_pairs={{0,4},{4,0},{8,12},{12,8},{16,20},{20,16},{24,28},{28,24},{1,5},{5... | collective-permute-start | bytes 393224 | tf_op jit(solution)/shard_map/ppermute | solution.py:326
  240.4 1.7 collective-permute-start.41
  242.0 1.3 collective-permute-start.43
  (29 other events, 347.2 us)
